TPU v7x, 128 devices: a whole 4x4x4 slice. The times are simulated.
128 devices in a mesh: dp: 16 (over x, z), vocab: 8 (over y, core).
Axes of the slice: x: 4, y: 4, z: 4, core: 2. Of those that a mesh axis runs over, the one named last changes fastest.
Arguments:
- hidden: bfloat16 [1024, 4096], P('dp', 'vocab'), may hold values from -400 to 400
- output_head_matrix: bfloat16 [4096, 151936], P(None, ('dp', 'vocab')), may hold values from -0.09375 to 0.09375
- row_counts: int32 [16], replicated, may hold values from 1 to 64, 512 in all
- token_ids: int32 [512], P('dp'), may hold values from 0 to 151935
- segment_ids: int32 [512], P('dp'), may hold values from 0 to 31, never falling along the last dimension, each value on 1 to 64 neighbouring positions
- cotangent: float32 [512], P('dp'), may hold values from -6 to 6
Outputs:
- logprobs: float32 [512], P('dp')
- grad_hidden: bfloat16 [1024, 4096], P('dp', 'vocab')
Inputs may be any that keep to these rules, and one draw needn't show every extreme that they name: `row_counts`: live rows of each index of dp; they sum to 512, one index holds 64. `segment_ids`: never falling; each segment has 1 to 64 positions, one exactly 64.
All inputs are finite; a program needn't handle non-finite values.
Results may differ from a plain program's by a relative error of at most 0.0034.
Values may be sent and summed in bfloat16 or wider, within the bound.
No kernel may reach another device: no remote copies, remote signals or barrier semaphores. Data moves between devices by JAX's collectives and lax.ppermute only.
A program may use at most 128 MiB of HBM per device.

v0:
```python
import functools

import jax
import jax.numpy as jnp
from jax import lax
from jax.experimental import pallas as pl
from jax.experimental.pallas import tpu as pltpu
from jax.sharding import PartitionSpec as P

freq_weight = 0.4
presence_weight = 0.8

N_DP, N_VOC = 16, 8
FEAT = 512
BF, F32, I32 = jnp.bfloat16, jnp.float32, jnp.int32
MIB = 1 << 20


def params(limit=32):
    return pltpu.CompilerParams(vmem_limit_bytes=limit * MIB)


def coords():
    dp, voc = lax.axis_index("dp"), lax.axis_index("vocab")
    return dp // 4, lax.rem(dp, 4), voc // 2, lax.rem(voc, 2)


def flat(x, z, y, c):
    return x * 32 + z * 8 + y * 2 + c


def shift_perm(axes, k):
    pairs = []
    for x in range(4):
        for z in range(4):
            for y in range(4):
                for c in range(2):
                    to = dict(x=x, z=z, y=y, c=c)
                    to[axes[c]] = (to[axes[c]] + k) % 4
                    pairs.append((flat(x, z, y, c), flat(**to)))
    return pairs


def pairing(axis, bits, cores=(0, 1)):
    pairs = []
    for x in range(4):
        for z in range(4):
            for y in range(4):
                for c in cores:
                    to = dict(x=x, z=z, y=y, c=c)
                    to[axis] ^= bits
                    pairs.append((flat(x, z, y, c), flat(**to)))
    return pairs


CORE_PERM = [(i, i ^ 1) for i in range(N_DP * N_VOC)]


def permute(v, pairs):
    return lax.ppermute(v, ("dp", "vocab"), pairs)


def iota(shape, dim):
    return lax.broadcasted_iota(I32, shape, dim)


VM = pl.BlockSpec(memory_space=pltpu.VMEM)
SM = pl.BlockSpec(memory_space=pltpu.SMEM)
HBM = pl.BlockSpec(memory_space=pltpu.HBM)


def my_start(rc_ref, dp):
    start = jnp.int32(0)
    for s in range(N_DP):
        start = start + jnp.where(s < dp, rc_ref[s], 0)
    return start


def pack_kernel(meta_ref, hid_ref, out_ref):
    dp = lax.axis_index("dp")
    counts = meta_ref[:, 0:16]
    lane = iota((1, 16), 1)
    start = jnp.sum(jnp.where(lane < dp, counts, 0.0), axis=1, keepdims=True).astype(I32)
    count = jnp.sum(jnp.where(lane == dp, counts, 0.0), axis=1, keepdims=True).astype(I32)
    row, col = iota((64, 64), 0), iota((64, 64), 1)
    target = (row >> 4) * 4 + (row & 3)
    src = ((row >> 2) & 3) * N_DP + ((target - start) & 15)
    sel = (col == src) & (col < count)
    rows = jnp.dot(sel.astype(F32).astype(BF), hid_ref[...], preferred_element_type=F32).astype(BF)
    kind = iota((8, 32), 0)
    tok = meta_ref[:, 16:48].astype(I32)
    cot = meta_ref[:, 80:112]
    digit = jnp.where(kind == 0, tok & 255, jnp.where(kind == 1, (tok >> 8) & 255, tok >> 16)).astype(F32)
    digit = jnp.where(kind == 3, meta_ref[:, 48:80], digit)
    high = cot.astype(BF).astype(F32)
    mid = (cot - high).astype(BF).astype(F32)
    low = cot - high - mid
    digit = jnp.where(kind < 4, digit, jnp.where(kind == 4, high, jnp.where(kind == 5, mid, low))).astype(BF)
    for a in range(N_DP):
        out_ref[a, 0:16, :] = rows[(a // 4) * 16:(a // 4) * 16 + 16]
        out_ref[a, 16:24, :] = jnp.zeros((8, FEAT), BF)
        out_ref[a, 16:24, 0:32] = digit


def placing(rc_ref, shape, slot_dim, per_source):
    x = lax.axis_index("dp") // 4
    k, row = iota(shape, slot_dim), iota(shape, 1 - slot_dim)
    s = k >> 4 if per_source == 16 else (k * 2731) >> 16
    u = k - s * per_source
    t, z = u >> 2, u & 3
    start = jnp.zeros(shape, I32)
    count = jnp.zeros(shape, I32)
    run = jnp.int32(0)
    for i in range(N_DP):
        start = jnp.where(s == i, run, start)
        count = jnp.where(s == i, rc_ref[i], count)
        run = run + rc_ref[i]
    a = x * 4 + z
    offset = (a - start) & 15
    base = (start + offset - a) >> 4
    sel = (u < 16) & (t * N_DP + offset < count) & (z * 32 + base + t == row)
    return sel.astype(F32).astype(BF)


def unpack_kernel(rc_ref, arr_ref, out_ref):
    sel = placing(rc_ref, (128, 384), 1, 24)
    out_ref[...] = jnp.dot(sel, arr_ref[...], preferred_element_type=F32).astype(BF)


def place_kernel(a0, a1, a2, a3, out_ref):
    x, z, y, c = coords()
    own = jnp.where(c == 0, x, y)
    for d, a in enumerate((a0, a1, a2, a3)):
        out_ref[pl.ds((own + d) & 3, 1)] = a[...][None]


def column(row):
    wide = jnp.broadcast_to(row, (128, row.shape[1]))
    return jnp.transpose(wide)[:, 0:1]


def code_kernel(cols, tok_ref, seg_ref, hit_ref, start_ref):
    dp, voc = lax.axis_index("dp"), lax.axis_index("vocab")
    tok, seg = tok_ref[...], seg_ref[...]
    tok_col = column(tok.astype(F32)).astype(I32)
    seg_col = column(seg.astype(F32)).astype(I32)
    prior = (seg_col == seg) & (iota((512, 512), 1) < iota((512, 512), 0))
    prior = prior.astype(F32).astype(BF)
    first = (dp * N_VOC + voc) * cols
    hits = (tok_col == first + iota((512, cols), 1)).astype(F32).astype(BF)
    hit_ref[...] = hits
    counts = jnp.dot(prior, hits, preferred_element_type=F32)
    start_ref[...] = -(freq_weight * counts) - presence_weight * (counts > 0).astype(F32)


def features(yy, core):
    return pl.ds(pl.multiple_of((yy * 2 + core) * FEAT, FEAT), FEAT)


def block_scores(ds, zero, one, head_ref, s_in, s_ref):
    x, z, y, c = coords()
    dims = (((1,), (1,)), ((), ()))
    if zero is not None:
        part = s_in[...]
        for d, block in zip(ds, zero):
            w = head_ref[:, features((y + d) & 3, 0)]
            part += lax.dot_general(block[...].reshape(512, FEAT), w, dims, preferred_element_type=F32)
        s_ref[...] = part
    else:
        s_ref[...] = s_in[...]
    if one is not None:
        def step(q, _):
            rows = jnp.concatenate([block[q] for block in one], axis=0)
            part = lax.dot_general(rows, head_ref[:, features(q, 1)], dims, preferred_element_type=F32)
            for i, d in enumerate(ds):
                s_ref[pl.ds(pl.multiple_of(((x + d) & 3) * 128, 128), 128), :] += part[i * 128:(i + 1) * 128]
            return _

        lax.fori_loop(0, 4, step, 0)


def both_scores(ds, own, other, head_ref, s_in, s_ref):
    c = coords()[3]

    @pl.when(c == 0)
    def _():
        block_scores(ds, own, other, head_ref, s_in, s_ref)

    @pl.when(c == 1)
    def _():
        block_scores(ds, other, own, head_ref, s_in, s_ref)


def first_scores_kernel(own, other, head_ref, s_in, s_ref):
    both_scores((0,), (own,), (other,), head_ref, s_in, s_ref)


def own_scores_kernel(a1, a2, a3, head_ref, s_in, s_ref):
    both_scores((1, 2, 3), (a1, a2, a3), None, head_ref, s_in, s_ref)


def last_scores_kernel(a1, a2, a3, head_ref, s_in, hit_ref, s_ref, exp_ref, stat_ref, ss):
    both_scores((1, 2, 3), None, (a1, a2, a3), head_ref, s_in, s_ref)

    def rows(i, _):
        at = pl.ds(pl.multiple_of(i * 32, 32), 32)
        s = s_ref[at, :]
        hit = hit_ref[at, :].astype(F32) > 0.5
        m = jnp.max(s, axis=1, keepdims=True)
        e = jnp.exp(s - m)
        exp_ref[at, :] = jnp.where(hit, 0.0, e).astype(BF)
        ss[at, 0:1] = m
        ss[at, 1:2] = jnp.sum(e, axis=1, keepdims=True)
        ss[at, 2:3] = jnp.sum(jnp.where(hit, s, 0.0), axis=1, keepdims=True)
        return _

    lax.fori_loop(0, 16, rows, 0, unroll=4)
    flat_stats = jnp.transpose(ss[...])
    for j in range(3):
        for k in range(4):
            piece = flat_stats[j:j + 1, k * 128:(k + 1) * 128]
            for n in range(N_VOC):
                stat_ref[n, j * 4 + k:j * 4 + k + 1, :] = piece
    for n in range(N_VOC):
        stat_ref[n, 12:16, :] = jnp.zeros((4, 128), F32)


def merge(st_ref, n):
    m = st_ref[0, 0:4, :]
    for i in range(1, n):
        m = jnp.maximum(m, st_ref[i, 0:4, :])
    total = jnp.zeros_like(m)
    picked = jnp.zeros_like(m)
    for i in range(n):
        total = total + st_ref[i, 4:8, :] * jnp.exp(st_ref[i, 0:4, :] - m)
        picked = picked + st_ref[i, 8:12, :]
    return m, total, picked


def merge_kernel(st_ref, out_ref, chip_ref):
    voc = lax.axis_index("vocab")
    m, total, picked = merge(st_ref, N_VOC)
    for n in range(N_DP):
        out_ref[n, 0:4, :] = m
        out_ref[n, 4:8, :] = total
        out_ref[n, 8:12, :] = picked
        out_ref[n, 12:16, :] = jnp.zeros((4, 128), F32)
    chip_ref[0:4, :] = st_ref[voc, 0:4, :]
    chip_ref[4:8, :] = st_ref[voc ^ 1, 0:4, :]


def long_row(v):
    return jnp.concatenate([v[k:k + 1, :] for k in range(4)], axis=1)


def columns(rows, out_ref):
    place = iota((128, rows[0].shape[1]), 0)
    wide = jnp.zeros(place.shape, F32)
    for i, row in enumerate(rows):
        wide = jnp.where(place == i, row, wide)
    out_ref[...] = jnp.transpose(wide)


def factor_kernel(st_ref, chip_ref, factor_ref, lp_ref, lps):
    x, z, y, c = coords()
    m, total, picked = merge(st_ref, N_DP)
    lps[0:4, :] = picked - m - jnp.log(total)
    mine = pltpu.roll(lps[pl.ds(x, 1), :], (128 - 32 * z) & 127, 1)
    lp_ref[...] = mine[:, 0:32]
    own, other = (jnp.exp(chip_ref[i:i + 4, :] - m) / total for i in (0, 4))
    columns([long_row(v) for v in (own, other, 1.0 - jnp.exp(picked - m) / total)], factor_ref)


def block_products(ds, core, left_ref, head_ref, put):
    x, z, y, c = coords()

    @pl.when(core == 0)
    def _():
        def one(i, d):
            v = jnp.dot(left_ref[...], head_ref[:, features((y + d) & 3, 0)], preferred_element_type=F32)
            for q in range(4):
                put(i, q, q * 128, v[q * 128:(q + 1) * 128])

        if ds == (0, 1, 2, 3):
            lax.fori_loop(0, 4, lambda d, _: one(d, d) or _, 0)
        else:
            for i, d in enumerate(ds):
                one(i, d)

    @pl.when(core == 1)
    def _():
        def step(q, _):
            ats = [pl.multiple_of(((x + d) & 3) * 128, 128) for d in ds]
            rows = jnp.concatenate([left_ref[pl.ds(at, 128), :] for at in ats], axis=0)
            v = jnp.dot(rows, head_ref[:, features(q, 1)], preferred_element_type=F32)
            for i, at in enumerate(ats):
                put(i, q, at, v[i * 128:(i + 1) * 128])
            return _

        lax.fori_loop(0, 4, step, 0)


def send_products_kernel(ds, left_ref, head_ref, *outs):
    def put(i, q, at, v):
        outs[i][q] = v.astype(BF)

    block_products(ds, 1 - coords()[3], left_ref, head_ref, put)


def target_products_kernel(left_ref, head_ref, send_ref, keep_ref):
    c = coords()[3]
    for core, out in ((1 - c, send_ref), (c, keep_ref)):
        def put(i, q, at, v, out=out):
            out[i, q] = v.astype(BF)

        block_products((0, 1, 2, 3), core, left_ref, head_ref, put)


def combine_kernel(ds, left_ref, head_ref, factor_ref, tk_ref, tg_ref, *refs):
    got, outs = refs[:len(ds)], refs[len(ds):]

    def put(i, q, at, v):
        f = factor_ref[pl.ds(at, 128), :]
        target = tk_ref[ds[i], q].astype(F32) + tg_ref[ds[i], q].astype(F32)
        v = target * f[:, 2:3] - (v * f[:, 0:1] + got[i][q].astype(F32) * f[:, 1:2])
        outs[i][q] = v.astype(outs[i].dtype)

    block_products(ds, coords()[3], left_ref, head_ref, put)


def ring_sum_kernel(own_in, r1, r2, r3, own_ref, b1, b2, b3):
    x, z, y, c = coords()
    own = jnp.where(c == 0, x, y)
    for d, out in enumerate((own_ref, b1, b2, b3)):
        q = (own + d) & 3
        out[...] = own_in[q] + r1[q].astype(F32) + r2[q].astype(F32) + r3[q].astype(F32)


def ways_kernel(rc_ref, cot_ref, back_ref, slot_ref, weight_ref):
    back_ref[...] = placing(rc_ref, (256, 128), 0, 16)
    dp = lax.axis_index("dp")
    start, count = my_start(rc_ref, dp), rc_ref[dp]
    j, k = iota((64, 256), 0), iota((64, 256), 1)
    a = (start + j) & 15
    sel = ((k >> 6) == (a >> 2)) & (((k >> 2) & 3) == (j >> 4)) & ((k & 3) == (a & 3)) & (j < count)
    slot_ref[...] = sel.astype(F32).astype(BF)
    g = start + iota((64, 512), 0)
    here = iota((64, 512), 1) == (g & 15) * 32 + (g >> 4)
    cot = jnp.sum(jnp.where(here, cot_ref[...], 0.0), axis=1, keepdims=True)
    weight_ref[...] = jnp.broadcast_to(cot, (64, 128))


def return_kernel(back_ref, own_in, r1, r2, r3, out_ref):
    v = (own_in[...] + r1[...] + r2[...] + r3[...]).astype(BF)
    out_ref[...] = jnp.dot(back_ref[...], v, preferred_element_type=F32).astype(BF)


def slots_kernel(slot_ref, weight_ref, arr_ref, out_ref):
    v = jnp.dot(slot_ref[...], arr_ref[...], preferred_element_type=F32)
    out_ref[...] = (v * weight_ref[:, 0:1]).astype(BF)


def sds(shape, dtype):
    return jax.ShapeDtypeStruct(shape, dtype)


def call(kernel, ins, outs, in_specs=None, scratch=(), limit=12, cost=None, aliases=None):
    multi = isinstance(outs, (list, tuple))
    return pl.pallas_call(
        kernel,
        out_shape=outs,
        in_specs=in_specs or [VM] * len(ins),
        out_specs=[VM] * len(outs) if multi else VM,
        scratch_shapes=list(scratch),
        compiler_params=params(limit),
        cost_estimate=cost,
        input_output_aliases=aliases or {},
    )(*ins)


def cost(flops, nbytes):
    return pl.CostEstimate(flops=flops, bytes_accessed=nbytes, transcendentals=0)


def per_device(hidden, head, row_counts, token_ids, segment_ids, cotangent):
    cols = head.shape[1]
    head = head.T
    meta = jnp.pad(row_counts, (0, 96)) + jnp.pad(token_ids, (16, 64)) + jnp.pad(segment_ids, (48, 32))
    meta = meta.astype(F32) + jnp.pad(cotangent, (80, 0))
    outgoing = call(pack_kernel, (meta.reshape(1, 112), hidden), sds((N_DP, 24, FEAT), BF))
    arrived = lax.all_to_all(outgoing, "dp", 0, 0, tiled=True)
    g1 = call(unpack_kernel, (row_counts, arrived.reshape(384, FEAT)), sds((128, FEAT), BF), in_specs=[SM, VM])
    digits = arrived[:, 16:24, 0:32].astype(F32)
    tokens = (digits[:, 0] + 256.0 * digits[:, 1] + 65536.0 * digits[:, 2]).astype(I32).reshape(1, 512)
    segments = digits[:, 3].astype(I32).reshape(1, 512)
    cots = (digits[:, 4] + digits[:, 5] + digits[:, 6]).reshape(1, 512)

    second = [g1] + [permute(g1, shift_perm("xy", 4 - d)) for d in (1, 2, 3)]
    hits, s = call(
        functools.partial(code_kernel, cols),
        (tokens, segments),
        [sds((512, cols), BF), sds((512, cols), F32)],
        cost=cost(1 << 20, 1 << 10),
    )
    second, s = lax.optimization_barrier((second, s))
    g2 = call(place_kernel, second, sds((4, 128, FEAT), BF))
    third = [g2] + [permute(g2, shift_perm("yx", 4 - d)) for d in (1, 2, 3)]

    wide = sds((512, cols), F32)
    small = cost(1 << 20, 1 << 10)
    quarter = sds((4, 128, FEAT), BF)
    pairs = ((1, 3), (2, 0))
    target_send, target_keep = call(
        target_products_kernel, (hits, head), [sds((4, 4, 128, FEAT), BF)] * 2, cost=small
    )
    other = permute(g2, CORE_PERM)
    s = call(first_scores_kernel, (g2, other, head, s), wide, cost=small, aliases={3: 0})
    *third, s, target_keep = lax.optimization_barrier((*third[1:], s, target_keep))
    other = [permute(v, CORE_PERM) for v in third]
    s = call(own_scores_kernel, (*third, head, s), wide, cost=small, aliases={4: 0})
    _, exps, stats = call(
        last_scores_kernel,
        (*other, head, s, hits),
        [wide, sds((512, cols), BF), sds((N_VOC, 16, 128), F32)],
        scratch=[pltpu.VMEM((512, 128), F32)],
        aliases={4: 0},
    )
    stats = lax.all_to_all(stats, "vocab", 0, 0, tiled=True)
    stats, chip = call(merge_kernel, (stats,), [sds((N_DP, 16, 128), F32), sds((8, 128), F32)])
    exps, chip, target_send = lax.optimization_barrier((exps, chip, target_send))
    target_got = permute(target_send, CORE_PERM)
    stats = lax.all_to_all(stats, "dp", 0, 0, tiled=True)
    got = {}
    for ds in pairs:
        out = call(functools.partial(send_products_kernel, ds), (exps, head), [quarter] * 2, cost=small)
        for d, v in zip(ds, out):
            got[d] = permute(v, CORE_PERM)
    factors, logprobs = call(
        factor_kernel, (stats, chip), [sds((512, 128), F32), sds((1, 32), F32)], scratch=[pltpu.VMEM((8, 128), F32)],
    )
    ring = {}
    for ds in pairs:
        out = call(
            functools.partial(combine_kernel, ds),
            (exps, head, factors, target_keep, target_got, *[got[d] for d in ds]),
            [quarter if d else sds((4, 128, FEAT), F32) for d in ds],
            cost=small,
        )
        for d, v in zip(ds, out):
            ring[d] = permute(v, shift_perm("yx", d)) if d else v
        factors, _ = lax.optimization_barrier((factors, out[0]))
    own, *out = call(ring_sum_kernel, [ring[d] for d in range(4)], [sds((128, FEAT), F32)] * 4)
    ring = [own] + [permute(v, shift_perm("xy", d + 1)) for d, v in enumerate(out)]
    back, slot, weight = call(
        ways_kernel,
        (row_counts, cots),
        [sds((256, 128), BF), sds((64, 256), BF), sds((64, 128), F32)],
        in_specs=[SM, VM],
        cost=small,
    )
    returning = call(return_kernel, (back, *ring), sds((256, FEAT), BF))
    returned = lax.all_to_all(returning.reshape(N_DP, 16, FEAT), "dp", 0, 0, tiled=True)
    grad_hidden = call(slots_kernel, (slot, weight, returned.reshape(256, FEAT)), sds((64, FEAT), BF))
    return logprobs.reshape(32), grad_hidden


def solution(mesh):
    return jax.shard_map(
        per_device,
        mesh=mesh,
        in_specs=(P("dp", "vocab"), P(None, ("dp", "vocab")), P(), P("dp"), P("dp"), P("dp")),
        out_specs=(P("dp"), P("dp", "vocab")),
        check_vma=False,
    )
```

profile of v0, /device:TPU:0, one launch (start us, length us, event | category | flops | bytes accessed | tf_op | source)
XLA Modules:
  0.0 130.9 jit_solution(15548131436064830891)
XLA Ops:
  2.5 17.6 %all_to_all.20 = bf16[16,24,512]{2,1,0:T(8,128)(2,1)S(1)} all-to-all(bf16[16,24,512]{2,1,0:T(8,128)(2,1)S(1)} %shard_map.77), channel_id=1, replica_groups=mesh['dp'=16,'vocab'=8] {'dp'}, dimensions={0} | all-to-all | bytes 786432 | tf_op jit(solution)/shard_map/all_to_all | solution.py:391
  21.5 1.4 %collective-permute-start = (bf16[128,512]{1,0:T(8,128)(2,1)S(1)}, bf16[128,512]{1,0:T(8,128)(2,1)S(1)}, u32[]{:S(2)}, u32[]{:S(2)}) collective-permute-start(bf16[128,512]{1,0:T(8,128)(2,1)S(1)} %shard_map.78.a0), channel_id=1, source_target_pairs={{0,96},{1,7},{2,98},{3,1},{4,100},{5,3},{6,102},{7,5},{8,104},{9,1... | collective-permute-start | bytes 393224 | tf_op jit(solution)/shard_map/ppermute | solution.py:60
  24.6 1.5 %shard_map.79 = (bf16[512,1187]{1,0:T(8,128)(2,1)S(1)}, f32[512,1187]{1,0:T(8,128)S(1)}) custom-call(s32[1,512]{1,0:T(1,128)S(1)} %convert_element_type.37.tok_ref, s32[1,512]{1,0:T(1,128)S(1)} %convert_element_type.39.seg_ref), custom_call_target="tpu_custom_call" | custom-call | flops 1048576 | bytes 1024 | tf_op jit(solution)/shard_map/pallas_call | solution.py:369
  26.5 2.9 %collective-permute-done.1.a2 = bf16[128,512]{1,0:T(8,128)(2,1)S(1)} collective-permute-done((bf16[128,512]{1,0:T(8,128)(2,1)S(1)}, bf16[128,512]{1,0:T(8,128)(2,1)S(1)}, u32[]{:S(2)}, u32[]{:S(2)}) %collective-permute-start.1) | collective-permute-done | bytes 131104 | tf_op jit(solution)/shard_map/ppermute | solution.py:60
  29.4 1.3 %collective-permute-done.2.a3 = bf16[128,512]{1,0:T(8,128)(2,1)S(1)} collective-permute-done((bf16[128,512]{1,0:T(8,128)(2,1)S(1)}, bf16[128,512]{1,0:T(8,128)(2,1)S(1)}, u32[]{:S(2)}, u32[]{:S(2)}) %collective-permute-start.2) | collective-permute-done | bytes 131104 | tf_op jit(solution)/shard_map/ppermute | solution.py:60
  30.9 3.1 %collective-permute-start.3 = (bf16[4,128,512]{2,1,0:T(8,128)(2,1)S(1)}, bf16[4,128,512]{2,1,0:T(8,128)(2,1)S(1)}, u32[]{:S(2)}, u32[]{:S(2)}) collective-permute-start(bf16[4,128,512]{2,1,0:T(8,128)(2,1)S(1)} %shard_map.80.own), channel_id=1, source_target_pairs={{0,6},{1,97},{2,0},{3,99},{4,2},{5,101},{6,4},{7,103},{8,14},{9,10... | collective-permute-start | bytes 1572872 | tf_op jit(solution)/shard_map/ppermute | solution.py:60
  35.6 3.8 %copy-done = bf16[4096,1187]{0,1:T(8,128)(2,1)S(1)} copy-done((bf16[4096,1187]{0,1:T(8,128)(2,1)S(1)}, bf16[4096,1187]{0,1:T(8,128)(2,1)}, u32[]{:S(2)}) %copy-start) | copy-done | bytes 9723928
  39.4 6.8 %shard_map.82 = (bf16[4,4,128,512]{3,2,1,0:T(8,128)(2,1)S(1)}, bf16[4,4,128,512]{3,2,1,0:T(8,128)(2,1)S(1)}) custom-call(bf16[512,1187]{1,0:T(8,128)(2,1)S(1)} %get-tuple-element.47.left_ref.hit_ref, bf16[1187,4096]{1,0:T(8,128)(2,1)S(1)} %bitcast.7), custom_call_target="tpu_custom_call" | custom-call | flops 1048576 | bytes 1024 | tf_op jit(solution)/shard_map/pallas_call | solution.py:369
  46.2 3.2 %shard_map.81.s_in = f32[512,1187]{1,0:T(8,128)S(1)} custom-call(bf16[4,128,512]{2,1,0:T(8,128)(2,1)S(1)} %shard_map.80.own, bf16[4,128,512]{2,1,0:T(8,128)(2,1)S(1)} %collective-permute-done.6.other, bf16[1187,4096]{1,0:T(8,128)(2,1)S(1)} %bitcast.8, f32[512,1187]{1,0:T(8,128)S(1)} %get-tuple-element.46.s_in), custom_call_target="tpu_custom_call", output_to_operand_aliasing={{}: (3, {})} | custom-call | flops 1048576 | bytes 1024 | tf_op jit(solution)/shard_map/pallas_call | solution.py:369
  50.8 2.8 %shard_map.83.s_in = f32[512,1187]{1,0:T(8,128)S(1)} custom-call(bf16[4,128,512]{2,1,0:T(8,128)(2,1)S(1)} %collective-permute-done.3.a1, bf16[4,128,512]{2,1,0:T(8,128)(2,1)S(1)} %collective-permute-done.4.a2, bf16[4,128,512]{2,1,0:T(8,128)(2,1)S(1)} %collective-permute-done.5.a3, bf16[1187,4096]{1,0:T(8,128)(2,1)S(1)} %bitcast.9, ...), custom_call_target="tpu_custom_call", output_to_operand_aliasing={{}: (4, {})} | custom-call | flops 1048576 | bytes 1024 | tf_op jit(solution)/shard_map/pallas_call | solution.py:369
  53.7 4.7 %shard_map.84 = (f32[512,1187]{1,0:T(8,128)S(1)}, bf16[512,1187]{1,0:T(8,128)(2,1)S(1)}, f32[8,16,128]{2,1,0:T(8,128)S(1)}) custom-call(bf16[4,128,512]{2,1,0:T(8,128)(2,1)S(1)} %collective-permute-done.7.a1, bf16[4,128,512]{2,1,0:T(8,128)(2,1)S(1)} %collective-permute-done.8.a2, ...), custom_call_target="tpu_custom_call", output_to_operand_aliasing={{0}: (4, {})} | custom-call | tf_op jit(solution)/shard_map/pallas_call | solution.py:369
  58.4 8.3 %all_to_all.21.st_ref = f32[8,16,128]{2,1,0:T(8,128)S(1)} all-to-all(f32[8,16,128]{2,1,0:T(8,128)S(1)} %get-tuple-element.53), channel_id=1, replica_groups=mesh['dp'=16,'vocab'=8] {'vocab'}, dimensions={0} | all-to-all | bytes 131072 | tf_op jit(solution)/shard_map/all_to_all | solution.py:428
  66.8 2.1 %shard_map.88 = (bf16[4,128,512]{2,1,0:T(8,128)(2,1)S(1)}, bf16[4,128,512]{2,1,0:T(8,128)(2,1)S(1)}) custom-call(bf16[512,1187]{1,0:T(8,128)(2,1)S(1)} %get-tuple-element.63.left_ref, bf16[1187,4096]{1,0:T(8,128)(2,1)S(1)} %bitcast.11), custom_call_target="tpu_custom_call" | custom-call | flops 1048576 | bytes 1024 | tf_op jit(solution)/shard_map/pallas_call | solution.py:369
  69.6 2.1 %shard_map.90 = (bf16[4,128,512]{2,1,0:T(8,128)(2,1)S(1)}, bf16[4,128,512]{2,1,0:T(8,128)(2,1)S(1)}) custom-call(bf16[512,1187]{1,0:T(8,128)(2,1)S(1)} %get-tuple-element.63.left_ref, bf16[1187,4096]{1,0:T(8,128)(2,1)S(1)} %bitcast.12), custom_call_target="tpu_custom_call" | custom-call | flops 1048576 | bytes 1024 | tf_op jit(solution)/shard_map/pallas_call | solution.py:369
  72.2 11.6 %all_to_all.22.st_ref = f32[16,16,128]{2,1,0:T(8,128)S(1)} all-to-all(f32[16,16,128]{2,1,0:T(8,128)S(1)} %get-tuple-element.54), channel_id=1, replica_groups=mesh['dp'=16,'vocab'=8] {'dp'}, dimensions={0} | all-to-all | bytes 262144 | tf_op jit(solution)/shard_map/all_to_all | solution.py:432
  84.5 1.8 %shard_map.89 = (bf16[4,128,512]{2,1,0:T(8,128)(2,1)S(1)}, bf16[4,128,512]{2,1,0:T(8,128)(2,1)S(1)}) custom-call(bf16[512,1187]{1,0:T(8,128)(2,1)S(1)} %get-tuple-element.63.left_ref, bf16[1187,4096]{1,0:T(8,128)(2,1)S(1)} %bitcast.13, f32[512,128]{1,0:T(8,128)S(1)} %get-tuple-element.70.factor_ref, bf16[4,4,128,512]{3,2,1,0:T(8,128)(2,1)S(1)} %get-tuple-element.65.tk_ref, ...), custom_call_target="tpu_custom_call" | custom-call | flops 1048576 | bytes 1024 | tf_op jit(solution)/shard_map/pallas_call | solution.py:369
  86.9 1.7 %shard_map.91 = (bf16[4,128,512]{2,1,0:T(8,128)(2,1)S(1)}, f32[4,128,512]{2,1,0:T(8,128)S(1)}) custom-call(bf16[512,1187]{1,0:T(8,128)(2,1)S(1)} %get-tuple-element.63.left_ref, bf16[1187,4096]{1,0:T(8,128)(2,1)S(1)} %bitcast.14, f32[512,128]{1,0:T(8,128)S(1)} %get-tuple-element.70.factor_ref, bf16[4,4,128,512]{3,2,1,0:T(8,128)(2,1)S(1)} %get-tuple-element.65.tk_ref, ...), custom_call_target="tpu_custom_call" | custom-call | flops 1048576 | bytes 1024 | tf_op jit(solution)/shard_map/pallas_call | solution.py:369
  88.6 2.2 %collective-permute-start.16 = (bf16[4,128,512]{2,1,0:T(8,128)(2,1)S(1)}, bf16[4,128,512]{2,1,0:T(8,128)(2,1)S(1)}, u32[]{:S(2)}, u32[]{:S(2)}) collective-permute-start(bf16[4,128,512]{2,1,0:T(8,128)(2,1)S(1)} %get-tuple-element.74), channel_id=1, source_target_pairs={{0,4},{1,65},{2,6},{3,67},{4,0},{5,69},{6,2},{7,71},{8,12},{9,73},... | collective-permute-start | bytes 1572872 | tf_op jit(solution)/shard_map/ppermute | solution.py:60
  91.8 10.1 %collective-permute-done.16.r2 = bf16[4,128,512]{2,1,0:T(8,128)(2,1)S(1)} collective-permute-done((bf16[4,128,512]{2,1,0:T(8,128)(2,1)S(1)}, bf16[4,128,512]{2,1,0:T(8,128)(2,1)S(1)}, u32[]{:S(2)}, u32[]{:S(2)}) %collective-permute-start.16) | collective-permute-done | bytes 524320 | tf_op jit(solution)/shard_map/ppermute | solution.py:60
  102.4 2.7 %collective-permute-done.17.r3 = bf16[4,128,512]{2,1,0:T(8,128)(2,1)S(1)} collective-permute-done((bf16[4,128,512]{2,1,0:T(8,128)(2,1)S(1)}, bf16[4,128,512]{2,1,0:T(8,128)(2,1)S(1)}, u32[]{:S(2)}, u32[]{:S(2)}) %collective-permute-start.17) | collective-permute-done | bytes 524320 | tf_op jit(solution)/shard_map/ppermute | solution.py:60
  105.8 2.1 %collective-permute-start.19 = (f32[128,512]{1,0:T(8,128)S(1)}, f32[128,512]{1,0:T(8,128)S(1)}, u32[]{:S(2)}, u32[]{:S(2)}) collective-permute-start(f32[128,512]{1,0:T(8,128)S(1)} %get-tuple-element.78), channel_id=1, source_target_pairs={{0,64},{1,5},{2,66},{3,7},{4,68},{5,1},{6,70},{7,3},{8,72},{9,13},... | collective-permute-start | bytes 786440 | tf_op jit(solution)/shard_map/ppermute | solution.py:60
  108.0 1.3 collective-permute-start.20
  110.4 5.4 %collective-permute-done.18.r1 = f32[128,512]{1,0:T(8,128)S(1)} collective-permute-done((f32[128,512]{1,0:T(8,128)S(1)}, f32[128,512]{1,0:T(8,128)S(1)}, u32[]{:S(2)}, u32[]{:S(2)}) %collective-permute-start.18) | collective-permute-done | bytes 262176 | tf_op jit(solution)/shard_map/ppermute | solution.py:60
  116.9 13.2 %all_to_all.23 = bf16[16,16,512]{2,1,0:T(8,128)(2,1)S(1)} all-to-all(bf16[16,16,512]{2,1,0:T(8,128)(2,1)S(1)} %bitcast.17), channel_id=1, replica_groups=mesh['dp'=16,'vocab'=8] {'dp'}, dimensions={0} | all-to-all | bytes 524288 | tf_op jit(solution)/shard_map/all_to_all | solution.py:462
  (57 shorter events, 16.5 us)
Async XLA Ops:
  21.5 5.0 %collective-permute-start = (bf16[128,512]{1,0:T(8,128)(2,1)S(1)}, bf16[128,512]{1,0:T(8,128)(2,1)S(1)}, u32[]{:S(2)}, u32[]{:S(2)}) collective-permute-start(bf16[128,512]{1,0:T(8,128)(2,1)S(1)} %shard_map.78.a0), channel_id=1, source_target_pairs={{0,96},{1,7},{2,98},{3,1},{4,100},{5,3},{6,102},{7,5},{8,104},{9,1... | collective-permute-start | bytes 393224 | tf_op jit(solution)/shard_map/ppermute | solution.py:60
  22.9 6.6 %collective-permute-start.1 = (bf16[128,512]{1,0:T(8,128)(2,1)S(1)}, bf16[128,512]{1,0:T(8,128)(2,1)S(1)}, u32[]{:S(2)}, u32[]{:S(2)}) collective-permute-start(bf16[128,512]{1,0:T(8,128)(2,1)S(1)} %shard_map.78.a0), channel_id=1, source_target_pairs={{0,64},{1,5},{2,66},{3,7},{4,68},{5,1},{6,70},{7,3},{8,72},{9,13},... | collective-permute-start | bytes 393224 | tf_op jit(solution)/shard_map/ppermute | solution.py:60
  23.7 7.1 %collective-permute-start.2 = (bf16[128,512]{1,0:T(8,128)(2,1)S(1)}, bf16[128,512]{1,0:T(8,128)(2,1)S(1)}, u32[]{:S(2)}, u32[]{:S(2)}) collective-permute-start(bf16[128,512]{1,0:T(8,128)(2,1)S(1)} %shard_map.78.a0), channel_id=1, source_target_pairs={{0,32},{1,3},{2,34},{3,5},{4,36},{5,7},{6,38},{7,1},{8,40},{9,11},... | collective-permute-start | bytes 393224 | tf_op jit(solution)/shard_map/ppermute | solution.py:60
  30.8 15.4 %collective-permute-start.6 = (bf16[4,128,512]{2,1,0:T(8,128)(2,1)S(1)}, bf16[4,128,512]{2,1,0:T(8,128)(2,1)S(1)}, u32[]{:S(2)}, u32[]{:S(2)}) collective-permute-start(bf16[4,128,512]{2,1,0:T(8,128)(2,1)S(1)} %shard_map.80.own), channel_id=1, source_target_pairs={{0,1},{1,0},{2,3},{3,2},{4,5},{5,4},{6,7},{7,6},{8,9},{9,8},{10,11... | collective-permute-start | bytes 1572872 | tf_op jit(solution)/shard_map/ppermute | solution.py:60
  30.9 18.5 %collective-permute-start.3 = (bf16[4,128,512]{2,1,0:T(8,128)(2,1)S(1)}, bf16[4,128,512]{2,1,0:T(8,128)(2,1)S(1)}, u32[]{:S(2)}, u32[]{:S(2)}) collective-permute-start(bf16[4,128,512]{2,1,0:T(8,128)(2,1)S(1)} %shard_map.80.own), channel_id=1, source_target_pairs={{0,6},{1,97},{2,0},{3,99},{4,2},{5,101},{6,4},{7,103},{8,14},{9,10... | collective-permute-start | bytes 1572872 | tf_op jit(solution)/shard_map/ppermute | solution.py:60
  34.0 15.4 %collective-permute-start.4 = (bf16[4,128,512]{2,1,0:T(8,128)(2,1)S(1)}, bf16[4,128,512]{2,1,0:T(8,128)(2,1)S(1)}, u32[]{:S(2)}, u32[]{:S(2)}) collective-permute-start(bf16[4,128,512]{2,1,0:T(8,128)(2,1)S(1)} %shard_map.80.own), channel_id=1, source_target_pairs={{0,4},{1,65},{2,6},{3,67},{4,0},{5,69},{6,2},{7,71},{8,12},{9,73},... | collective-permute-start | bytes 1572872 | tf_op jit(solution)/shard_map/ppermute | solution.py:60
  34.6 15.7 %collective-permute-start.5 = (bf16[4,128,512]{2,1,0:T(8,128)(2,1)S(1)}, bf16[4,128,512]{2,1,0:T(8,128)(2,1)S(1)}, u32[]{:S(2)}, u32[]{:S(2)}) collective-permute-start(bf16[4,128,512]{2,1,0:T(8,128)(2,1)S(1)} %shard_map.80.own), channel_id=1, source_target_pairs={{0,2},{1,33},{2,4},{3,35},{4,6},{5,37},{6,0},{7,39},{8,10},{9,41},... | collective-permute-start | bytes 1572872 | tf_op jit(solution)/shard_map/ppermute | solution.py:60
  35.6 3.8 %copy-start = (bf16[4096,1187]{0,1:T(8,128)(2,1)S(1)}, bf16[4096,1187]{0,1:T(8,128)(2,1)}, u32[]{:S(2)}) copy-start(bf16[4096,1187]{0,1:T(8,128)(2,1)} %param.7) | copy-start | bytes 29171716
  39.4 6.8 %copy-start.1 = (bf16[4096,1187]{0,1:T(8,128)(2,1)S(1)}, bf16[4096,1187]{0,1:T(8,128)(2,1)}, u32[]{:S(2)}) copy-start(bf16[4096,1187]{0,1:T(8,128)(2,1)} %param.7) | copy-start | bytes 29171716
  50.3 3.3 %collective-permute-start.7 = (bf16[4,128,512]{2,1,0:T(8,128)(2,1)S(1)}, bf16[4,128,512]{2,1,0:T(8,128)(2,1)S(1)}, u32[]{:S(2)}, u32[]{:S(2)}) collective-permute-start(bf16[4,128,512]{2,1,0:T(8,128)(2,1)S(1)} %collective-permute-done.3.a1), channel_id=1, source_target_pairs={{0,1},{1,0},{2,3},{3,2},{4,5},{5,4},{6,7},{7,6},{8,9},{9,8},{10,11... | collective-permute-start | bytes 1572872 | tf_op jit(solution)/shard_map/ppermute | solution.py:60
  50.3 3.3 %collective-permute-start.8 = (bf16[4,128,512]{2,1,0:T(8,128)(2,1)S(1)}, bf16[4,128,512]{2,1,0:T(8,128)(2,1)S(1)}, u32[]{:S(2)}, u32[]{:S(2)}) collective-permute-start(bf16[4,128,512]{2,1,0:T(8,128)(2,1)S(1)} %collective-permute-done.4.a2), channel_id=1, source_target_pairs={{0,1},{1,0},{2,3},{3,2},{4,5},{5,4},{6,7},{7,6},{8,9},{9,8},{10,11... | collective-permute-start | bytes 1572872 | tf_op jit(solution)/shard_map/ppermute | solution.py:60
  50.8 2.9 %collective-permute-start.9 = (bf16[4,128,512]{2,1,0:T(8,128)(2,1)S(1)}, bf16[4,128,512]{2,1,0:T(8,128)(2,1)S(1)}, u32[]{:S(2)}, u32[]{:S(2)}) collective-permute-start(bf16[4,128,512]{2,1,0:T(8,128)(2,1)S(1)} %collective-permute-done.5.a3), channel_id=1, source_target_pairs={{0,1},{1,0},{2,3},{3,2},{4,5},{5,4},{6,7},{7,6},{8,9},{9,8},{10,11... | collective-permute-start | bytes 1572872 | tf_op jit(solution)/shard_map/ppermute | solution.py:60
  66.8 17.8 %collective-permute-start.10 = (bf16[4,4,128,512]{3,2,1,0:T(8,128)(2,1)S(1)}, bf16[4,4,128,512]{3,2,1,0:T(8,128)(2,1)S(1)}, u32[]{:S(2)}, u32[]{:S(2)}) collective-permute-start(bf16[4,4,128,512]{3,2,1,0:T(8,128)(2,1)S(1)} %get-tuple-element.66), channel_id=1, source_target_pairs={{0,1},{1,0},{2,3},{3,2},{4,5},{5,4},{6,7},{7,6},{8,9},{9,8},{10,11... | collective-permute-start | bytes 6291464 | tf_op jit(solution)/shard_map/ppermute | solution.py:60
  69.0 15.6 %collective-permute-start.11 = (bf16[4,128,512]{2,1,0:T(8,128)(2,1)S(1)}, bf16[4,128,512]{2,1,0:T(8,128)(2,1)S(1)}, u32[]{:S(2)}, u32[]{:S(2)}) collective-permute-start(bf16[4,128,512]{2,1,0:T(8,128)(2,1)S(1)} %get-tuple-element.67), channel_id=1, source_target_pairs={{0,1},{1,0},{2,3},{3,2},{4,5},{5,4},{6,7},{7,6},{8,9},{9,8},{10,11... | collective-permute-start | bytes 1572872 | tf_op jit(solution)/shard_map/ppermute | solution.py:60
  69.1 15.5 %collective-permute-start.12 = (bf16[4,128,512]{2,1,0:T(8,128)(2,1)S(1)}, bf16[4,128,512]{2,1,0:T(8,128)(2,1)S(1)}, u32[]{:S(2)}, u32[]{:S(2)}) collective-permute-start(bf16[4,128,512]{2,1,0:T(8,128)(2,1)S(1)} %get-tuple-element.68), channel_id=1, source_target_pairs={{0,1},{1,0},{2,3},{3,2},{4,5},{5,4},{6,7},{7,6},{8,9},{9,8},{10,11... | collective-permute-start | bytes 1572872 | tf_op jit(solution)/shard_map/ppermute | solution.py:60
  71.7 15.3 %collective-permute-start.13 = (bf16[4,128,512]{2,1,0:T(8,128)(2,1)S(1)}, bf16[4,128,512]{2,1,0:T(8,128)(2,1)S(1)}, u32[]{:S(2)}, u32[]{:S(2)}) collective-permute-start(bf16[4,128,512]{2,1,0:T(8,128)(2,1)S(1)} %get-tuple-element.71), channel_id=1, source_target_pairs={{0,1},{1,0},{2,3},{3,2},{4,5},{5,4},{6,7},{7,6},{8,9},{9,8},{10,11... | collective-permute-start | bytes 1572872 | tf_op jit(solution)/shard_map/ppermute | solution.py:60
  71.7 15.2 %collective-permute-start.14 = (bf16[4,128,512]{2,1,0:T(8,128)(2,1)S(1)}, bf16[4,128,512]{2,1,0:T(8,128)(2,1)S(1)}, u32[]{:S(2)}, u32[]{:S(2)}) collective-permute-start(bf16[4,128,512]{2,1,0:T(8,128)(2,1)S(1)} %get-tuple-element.72), channel_id=1, source_target_pairs={{0,1},{1,0},{2,3},{3,2},{4,5},{5,4},{6,7},{7,6},{8,9},{9,8},{10,11... | collective-permute-start | bytes 1572872 | tf_op jit(solution)/shard_map/ppermute | solution.py:60
  86.3 16.1 %collective-permute-start.15 = (bf16[4,128,512]{2,1,0:T(8,128)(2,1)S(1)}, bf16[4,128,512]{2,1,0:T(8,128)(2,1)S(1)}, u32[]{:S(2)}, u32[]{:S(2)}) collective-permute-start(bf16[4,128,512]{2,1,0:T(8,128)(2,1)S(1)} %get-tuple-element.69), channel_id=1, source_target_pairs={{0,2},{1,33},{2,4},{3,35},{4,6},{5,37},{6,0},{7,39},{8,10},{9,41},... | collective-permute-start | bytes 1572872 | tf_op jit(solution)/shard_map/ppermute | solution.py:60
  88.6 20.8 %copy-start.4 = (s32[16]{0:T(128)S(1)}, s32[16]{0:T(128)}, u32[]{:S(2)}) copy-start(s32[16]{0:T(128)} %rc_ref.3) | copy-start | bytes 196
  88.6 13.3 %collective-permute-start.16 = (bf16[4,128,512]{2,1,0:T(8,128)(2,1)S(1)}, bf16[4,128,512]{2,1,0:T(8,128)(2,1)S(1)}, u32[]{:S(2)}, u32[]{:S(2)}) collective-permute-start(bf16[4,128,512]{2,1,0:T(8,128)(2,1)S(1)} %get-tuple-element.74), channel_id=1, source_target_pairs={{0,4},{1,65},{2,6},{3,67},{4,0},{5,69},{6,2},{7,71},{8,12},{9,73},... | collective-permute-start | bytes 1572872 | tf_op jit(solution)/shard_map/ppermute | solution.py:60
  90.8 14.3 %collective-permute-start.17 = (bf16[4,128,512]{2,1,0:T(8,128)(2,1)S(1)}, bf16[4,128,512]{2,1,0:T(8,128)(2,1)S(1)}, u32[]{:S(2)}, u32[]{:S(2)}) collective-permute-start(bf16[4,128,512]{2,1,0:T(8,128)(2,1)S(1)} %get-tuple-element.75), channel_id=1, source_target_pairs={{0,6},{1,97},{2,0},{3,99},{4,2},{5,101},{6,4},{7,103},{8,14},{9,10... | collective-permute-start | bytes 1572872 | tf_op jit(solution)/shard_map/ppermute | solution.py:60
  105.3 10.5 %collective-permute-start.18 = (f32[128,512]{1,0:T(8,128)S(1)}, f32[128,512]{1,0:T(8,128)S(1)}, u32[]{:S(2)}, u32[]{:S(2)}) collective-permute-start(f32[128,512]{1,0:T(8,128)S(1)} %get-tuple-element.77), channel_id=1, source_target_pairs={{0,32},{1,3},{2,34},{3,5},{4,36},{5,7},{6,38},{7,1},{8,40},{9,11},... | collective-permute-start | bytes 786440 | tf_op jit(solution)/shard_map/ppermute | solution.py:60
  105.8 9.9 %collective-permute-start.19 = (f32[128,512]{1,0:T(8,128)S(1)}, f32[128,512]{1,0:T(8,128)S(1)}, u32[]{:S(2)}, u32[]{:S(2)}) collective-permute-start(f32[128,512]{1,0:T(8,128)S(1)} %get-tuple-element.78), channel_id=1, source_target_pairs={{0,64},{1,5},{2,66},{3,7},{4,68},{5,1},{6,70},{7,3},{8,72},{9,13},... | collective-permute-start | bytes 786440 | tf_op jit(solution)/shard_map/ppermute | solution.py:60
  108.0 8.7 %collective-permute-start.20 = (f32[128,512]{1,0:T(8,128)S(1)}, f32[128,512]{1,0:T(8,128)S(1)}, u32[]{:S(2)}, u32[]{:S(2)}) collective-permute-start(f32[128,512]{1,0:T(8,128)S(1)} %get-tuple-element.79), channel_id=1, source_target_pairs={{0,96},{1,7},{2,98},{3,1},{4,100},{5,3},{6,102},{7,5},{8,104},{9,1... | collective-permute-start | bytes 786440 | tf_op jit(solution)/shard_map/ppermute | solution.py:60
  (2 other events, 1.5 us)
where the time goes:
time: 131 us
  blocking collectives  50.7 us (39%)
  Pallas kernels  30.7 us (23%)
  waiting for transfers between devices  25.2 us (19%)
  starting transfers between devices  17.1 us (13%)
  local copies, waits for them, and re-layouts  5.52 us (4%)
    pallas_call x18, Pallas kernels, call(): pl.pallas_call(kernel, out_shape=outs, in_specs=in_specs or [VM] * len(in...  30.7 us
    ppermute x21, waiting for transfers between devices, permute(): return lax.ppermute(v, ('dp', 'vocab'), pairs)  25.2 us
    all_to_all x1, blocking collectives, per_device(): arrived = lax.all_to_all(outgoing, 'dp', 0, 0, tiled=True)  17.6 us
    ppermute x21, starting transfers between devices, permute(): return lax.ppermute(v, ('dp', 'vocab'), pairs)  17.1 us
    all_to_all x1, blocking collectives, per_device(): lax.all_to_all(returning.reshape(N_DP, 16, FEAT), 'dp', 0, 0, tiled=True)  13.2 us
    all_to_all x1, blocking collectives, per_device(): stats = lax.all_to_all(stats, 'dp', 0, 0, tiled=True)  11.6 us
    all_to_all x1, blocking collectives, per_device(): stats = lax.all_to_all(stats, 'vocab', 0, 0, tiled=True)  8.29 us
    unnamed x10, local copies, waits for them, and re-layouts  5.29 us
  transfers between devices with their start and end apart: 21, of which 10 were waited for; matrix products, arithmetic and copies ran while one was open for 0% of the time, Pallas kernels for 18%

commit v1 on v0

--- a/solution.py
+++ b/solution.py
@@ -65,23 +65,18 @@
 
 
 VM = pl.BlockSpec(memory_space=pltpu.VMEM)
-SM = pl.BlockSpec(memory_space=pltpu.SMEM)
-HBM = pl.BlockSpec(memory_space=pltpu.HBM)
-
-
-def my_start(rc_ref, dp):
-    start = jnp.int32(0)
-    for s in range(N_DP):
-        start = start + jnp.where(s < dp, rc_ref[s], 0)
-    return start
+
+
+def my_slots(meta_ref):
+    dp = lax.axis_index("dp")
+    counts, lane = meta_ref[:, 0:16], iota((1, 16), 1)
+    start = jnp.sum(jnp.where(lane < dp, counts, 0.0), axis=1, keepdims=True)
+    count = jnp.sum(jnp.where(lane == dp, counts, 0.0), axis=1, keepdims=True)
+    return start.astype(I32), count.astype(I32)
 
 
 def pack_kernel(meta_ref, hid_ref, out_ref):
-    dp = lax.axis_index("dp")
-    counts = meta_ref[:, 0:16]
-    lane = iota((1, 16), 1)
-    start = jnp.sum(jnp.where(lane < dp, counts, 0.0), axis=1, keepdims=True).astype(I32)
-    count = jnp.sum(jnp.where(lane == dp, counts, 0.0), axis=1, keepdims=True).astype(I32)
+    start, count = my_slots(meta_ref)
     row, col = iota((64, 64), 0), iota((64, 64), 1)
     target = (row >> 4) * 4 + (row & 3)
     src = ((row >> 2) & 3) * N_DP + ((target - start) & 15)
@@ -102,28 +97,29 @@
         out_ref[a, 16:24, 0:32] = digit
 
 
-def placing(rc_ref, shape, slot_dim, per_source):
+def placing(meta_ref, shape, slot_dim, per_source):
     x = lax.axis_index("dp") // 4
-    k, row = iota(shape, slot_dim), iota(shape, 1 - slot_dim)
+    line = (shape[0], 1) if slot_dim == 0 else (1, shape[1])
+    k, row = iota(line, slot_dim), iota(shape, 1 - slot_dim)
     s = k >> 4 if per_source == 16 else (k * 2731) >> 16
     u = k - s * per_source
     t, z = u >> 2, u & 3
-    start = jnp.zeros(shape, I32)
-    count = jnp.zeros(shape, I32)
-    run = jnp.int32(0)
+    start = jnp.zeros(line, F32)
+    count = jnp.zeros(line, F32)
     for i in range(N_DP):
-        start = jnp.where(s == i, run, start)
-        count = jnp.where(s == i, rc_ref[i], count)
-        run = run + rc_ref[i]
+        live = meta_ref[:, i:i + 1]
+        start = start + jnp.where(s > i, live, 0.0)
+        count = jnp.where(s == i, live, count)
+    start, count = start.astype(I32), count.astype(I32)
     a = x * 4 + z
     offset = (a - start) & 15
     base = (start + offset - a) >> 4
-    sel = (u < 16) & (t * N_DP + offset < count) & (z * 32 + base + t == row)
-    return sel.astype(F32).astype(BF)
-
-
-def unpack_kernel(rc_ref, arr_ref, out_ref):
-    sel = placing(rc_ref, (128, 384), 1, 24)
+    at = jnp.where((u < 16) & (t * N_DP + offset < count), z * 32 + base + t, -1)
+    return (at == row).astype(F32).astype(BF)
+
+
+def unpack_kernel(meta_ref, arr_ref, out_ref):
+    sel = placing(meta_ref, (128, 384), 1, 24)
     out_ref[...] = jnp.dot(sel, arr_ref[...], preferred_element_type=F32).astype(BF)
 
 
@@ -218,35 +214,30 @@
     flat_stats = jnp.transpose(ss[...])
     for j in range(3):
         for k in range(4):
-            piece = flat_stats[j:j + 1, k * 128:(k + 1) * 128]
-            for n in range(N_VOC):
-                stat_ref[n, j * 4 + k:j * 4 + k + 1, :] = piece
-    for n in range(N_VOC):
-        stat_ref[n, 12:16, :] = jnp.zeros((4, 128), F32)
-
-
-def merge(st_ref, n):
-    m = st_ref[0, 0:4, :]
-    for i in range(1, n):
-        m = jnp.maximum(m, st_ref[i, 0:4, :])
-    total = jnp.zeros_like(m)
-    picked = jnp.zeros_like(m)
-    for i in range(n):
-        total = total + st_ref[i, 4:8, :] * jnp.exp(st_ref[i, 0:4, :] - m)
-        picked = picked + st_ref[i, 8:12, :]
-    return m, total, picked
-
-
-def merge_kernel(st_ref, out_ref, chip_ref):
-    voc = lax.axis_index("vocab")
-    m, total, picked = merge(st_ref, N_VOC)
+            stat_ref[j * 4 + k:j * 4 + k + 1, :] = flat_stats[j:j + 1, k * 128:(k + 1) * 128]
+    stat_ref[12:16, :] = jnp.zeros((4, 128), F32)
+
+
+def merge(found):
+    m = functools.reduce(jnp.maximum, [st[0:4, :] for st in found])
+    total = sum(st[4:8, :] * jnp.exp(st[0:4, :] - m) for st in found)
+    return m, total, sum(st[8:12, :] for st in found)
+
+
+def chip_kernel(a_ref, b_ref, out_ref, chip_ref):
+    out_ref[0:4, :], out_ref[4:8, :], out_ref[8:12, :] = merge((a_ref, b_ref))
+    out_ref[12:16, :] = jnp.zeros((4, 128), F32)
+    chip_ref[0:4, :] = a_ref[0:4, :]
+    chip_ref[4:8, :] = b_ref[0:4, :]
+
+
+def line_kernel(s0, s1, s2, s3, out_ref):
+    m, total, picked = merge((s0, s1, s2, s3))
     for n in range(N_DP):
         out_ref[n, 0:4, :] = m
         out_ref[n, 4:8, :] = total
         out_ref[n, 8:12, :] = picked
         out_ref[n, 12:16, :] = jnp.zeros((4, 128), F32)
-    chip_ref[0:4, :] = st_ref[voc, 0:4, :]
-    chip_ref[4:8, :] = st_ref[voc ^ 1, 0:4, :]
 
 
 def long_row(v):
@@ -263,7 +254,7 @@
 
 def factor_kernel(st_ref, chip_ref, factor_ref, lp_ref, lps):
     x, z, y, c = coords()
-    m, total, picked = merge(st_ref, N_DP)
+    m, total, picked = merge([st_ref.at[n] for n in range(N_DP)])
     lps[0:4, :] = picked - m - jnp.log(total)
     mine = pltpu.roll(lps[pl.ds(x, 1), :], (128 - 32 * z) & 127, 1)
     lp_ref[...] = mine[:, 0:32]
@@ -336,10 +327,9 @@
         out[...] = own_in[q] + r1[q].astype(F32) + r2[q].astype(F32) + r3[q].astype(F32)
 
 
-def ways_kernel(rc_ref, cot_ref, back_ref, slot_ref, weight_ref):
-    back_ref[...] = placing(rc_ref, (256, 128), 0, 16)
-    dp = lax.axis_index("dp")
-    start, count = my_start(rc_ref, dp), rc_ref[dp]
+def ways_kernel(meta_ref, cot_ref, back_ref, slot_ref, weight_ref):
+    back_ref[...] = placing(meta_ref, (256, 128), 0, 16)
+    start, count = my_slots(meta_ref)
     j, k = iota((64, 256), 0), iota((64, 256), 1)
     a = (start + j) & 15
     sel = ((k >> 6) == (a >> 2)) & (((k >> 2) & 3) == (j >> 4)) & ((k & 3) == (a & 3)) & (j < count)
@@ -387,9 +377,10 @@
     head = head.T
     meta = jnp.pad(row_counts, (0, 96)) + jnp.pad(token_ids, (16, 64)) + jnp.pad(segment_ids, (48, 32))
     meta = meta.astype(F32) + jnp.pad(cotangent, (80, 0))
-    outgoing = call(pack_kernel, (meta.reshape(1, 112), hidden), sds((N_DP, 24, FEAT), BF))
+    meta = meta.reshape(1, 112)
+    outgoing = call(pack_kernel, (meta, hidden), sds((N_DP, 24, FEAT), BF))
     arrived = lax.all_to_all(outgoing, "dp", 0, 0, tiled=True)
-    g1 = call(unpack_kernel, (row_counts, arrived.reshape(384, FEAT)), sds((128, FEAT), BF), in_specs=[SM, VM])
+    g1 = call(unpack_kernel, (meta, arrived.reshape(384, FEAT)), sds((128, FEAT), BF))
     digits = arrived[:, 16:24, 0:32].astype(F32)
     tokens = (digits[:, 0] + 256.0 * digits[:, 1] + 65536.0 * digits[:, 2]).astype(I32).reshape(1, 512)
     segments = digits[:, 3].astype(I32).reshape(1, 512)
@@ -421,20 +412,23 @@
     _, exps, stats = call(
         last_scores_kernel,
         (*other, head, s, hits),
-        [wide, sds((512, cols), BF), sds((N_VOC, 16, 128), F32)],
+        [wide, sds((512, cols), BF), sds((16, 128), F32)],
         scratch=[pltpu.VMEM((512, 128), F32)],
         aliases={4: 0},
     )
-    stats = lax.all_to_all(stats, "vocab", 0, 0, tiled=True)
-    stats, chip = call(merge_kernel, (stats,), [sds((N_DP, 16, 128), F32), sds((8, 128), F32)])
-    exps, chip, target_send = lax.optimization_barrier((exps, chip, target_send))
+    stats, chip = call(
+        chip_kernel, (stats, permute(stats, CORE_PERM)), [sds((16, 128), F32), sds((8, 128), F32)]
+    )
+    line = [stats] + [permute(stats, shift_perm("yy", d)) for d in (1, 2, 3)]
+    send = {}
+    for ds in pairs:
+        out = call(functools.partial(send_products_kernel, ds), (exps, head), [quarter] * 2, cost=small)
+        send.update(zip(ds, out))
+    line, send, target_send = lax.optimization_barrier((line, send, target_send))
+    stats = call(line_kernel, line, sds((N_DP, 16, 128), F32))
+    got = {d: permute(send[d], CORE_PERM) for d in (1, 3, 2, 0)}
     target_got = permute(target_send, CORE_PERM)
     stats = lax.all_to_all(stats, "dp", 0, 0, tiled=True)
-    got = {}
-    for ds in pairs:
-        out = call(functools.partial(send_products_kernel, ds), (exps, head), [quarter] * 2, cost=small)
-        for d, v in zip(ds, out):
-            got[d] = permute(v, CORE_PERM)
     factors, logprobs = call(
         factor_kernel, (stats, chip), [sds((512, 128), F32), sds((1, 32), F32)], scratch=[pltpu.VMEM((8, 128), F32)],
     )
@@ -444,7 +438,7 @@
             functools.partial(combine_kernel, ds),
             (exps, head, factors, target_keep, target_got, *[got[d] for d in ds]),
             [quarter if d else sds((4, 128, FEAT), F32) for d in ds],
-            cost=small,
+            cost=cost(3 << 30, 1 << 10),
         )
         for d, v in zip(ds, out):
             ring[d] = permute(v, shift_perm("yx", d)) if d else v
@@ -453,9 +447,8 @@
     ring = [own] + [permute(v, shift_perm("xy", d + 1)) for d, v in enumerate(out)]
     back, slot, weight = call(
         ways_kernel,
-        (row_counts, cots),
+        (meta, cots),
         [sds((256, 128), BF), sds((64, 256), BF), sds((64, 128), F32)],
-        in_specs=[SM, VM],
         cost=small,
     )
     returning = call(return_kernel, (back, *ring), sds((256, FEAT), BF))

time: 131 us -> 127 us (0.969)
  blocking collectives: 50.7 us -> 42.8 us
  starting transfers between devices: 17.1 us -> 21.6 us
    all_to_all x1 -> x0, blocking collectives: 8.29 us -> none  [per_device(): stats = lax.all_to_all(stats, 'vocab', 0, 0, tiled=True)]
    ppermute x21 -> x25, starting transfers between devices: 17.1 us -> 21.6 us  [permute(): return lax.ppermute(v, ('dp', 'vocab'), pairs)]
    unnamed x10 -> x6, local copies, waits for them, and re-layouts: 5.29 us -> 4.62 us
    ppermute x21 -> x25, waiting for transfers between devices: 25.2 us -> 25.5 us  [permute(): return lax.ppermute(v, ('dp', 'vocab'), pairs)]
    pallas_call x18 -> x19, Pallas kernels: 30.7 us -> 30.5 us  [call(): pl.pallas_call(kernel, out_shape=outs, in_specs=in_specs or [VM] * len(in...]
  transfers between devices with their start and end apart: 21 -> 25, of which waited for: 10 -> 11; matrix products, arithmetic and copies ran while one was open for 0% -> 0% of each run, Pallas kernels for 18% -> 19%
where the time goes in v1:
time: 127 us
  blocking collectives  42.8 us (34%)
  Pallas kernels  30.5 us (24%)
  waiting for transfers between devices  25.5 us (20%)
  starting transfers between devices  21.6 us (17%)
  local copies, waits for them, and re-layouts  4.86 us (4%)
    pallas_call x19, Pallas kernels, call(): pl.pallas_call(kernel, out_shape=outs, in_specs=in_specs or [VM] * len(in...  30.5 us
    ppermute x25, waiting for transfers between devices, permute(): return lax.ppermute(v, ('dp', 'vocab'), pairs)  25.5 us
    ppermute x25, starting transfers between devices, permute(): return lax.ppermute(v, ('dp', 'vocab'), pairs)  21.6 us
    all_to_all x1, blocking collectives, per_device(): arrived = lax.all_to_all(outgoing, 'dp', 0, 0, tiled=True)  17.6 us
    all_to_all x1, blocking collectives, per_device(): lax.all_to_all(returning.reshape(N_DP, 16, FEAT), 'dp', 0, 0, tiled=True)  13.2 us
    all_to_all x1, blocking collectives, per_device(): stats = lax.all_to_all(stats, 'dp', 0, 0, tiled=True)  12 us
    unnamed x6, local copies, waits for them, and re-layouts  4.62 us
  transfers between devices with their start and end apart: 25, of which 11 were waited for; matrix products, arithmetic and copies ran while one was open for 0% of the time, Pallas kernels for 19%

profile of v1, /device:TPU:0, one launch (start us, length us, event | category | flops | bytes accessed | tf_op | source)
XLA Modules:
  0.0 127.0 jit_solution(8192013463488678708)
XLA Ops:
  2.5 17.6 %all_to_all.15 = bf16[16,24,512]{2,1,0:T(8,128)(2,1)S(1)} all-to-all(bf16[16,24,512]{2,1,0:T(8,128)(2,1)S(1)} %shard_map.77), channel_id=1, replica_groups=mesh['dp'=16,'vocab'=8] {'dp'}, dimensions={0} | all-to-all | bytes 786432 | tf_op jit(solution)/shard_map/all_to_all | solution.py:382
  20.4 1.4 %collective-permute-start = (bf16[128,512]{1,0:T(8,128)(2,1)S(1)}, bf16[128,512]{1,0:T(8,128)(2,1)S(1)}, u32[]{:S(2)}, u32[]{:S(2)}) collective-permute-start(bf16[128,512]{1,0:T(8,128)(2,1)S(1)} %shard_map.78.a0), channel_id=1, source_target_pairs={{0,96},{1,7},{2,98},{3,1},{4,100},{5,3},{6,102},{7,5},{8,104},{9,1... | collective-permute-start | bytes 393224 | tf_op jit(solution)/shard_map/ppermute | solution.py:60
  23.4 1.5 %shard_map.79 = (bf16[512,1187]{1,0:T(8,128)(2,1)S(1)}, f32[512,1187]{1,0:T(8,128)S(1)}) custom-call(s32[1,512]{1,0:T(1,128)S(1)} %convert_element_type.37.tok_ref, s32[1,512]{1,0:T(1,128)S(1)} %convert_element_type.39.seg_ref), custom_call_target="tpu_custom_call" | custom-call | flops 1048576 | bytes 1024 | tf_op jit(solution)/shard_map/pallas_call | solution.py:359
  25.4 2.9 %collective-permute-done.1.a2 = bf16[128,512]{1,0:T(8,128)(2,1)S(1)} collective-permute-done((bf16[128,512]{1,0:T(8,128)(2,1)S(1)}, bf16[128,512]{1,0:T(8,128)(2,1)S(1)}, u32[]{:S(2)}, u32[]{:S(2)}) %collective-permute-start.1) | collective-permute-done | bytes 131104 | tf_op jit(solution)/shard_map/ppermute | solution.py:60
  29.8 3.1 %collective-permute-start.3 = (bf16[4,128,512]{2,1,0:T(8,128)(2,1)S(1)}, bf16[4,128,512]{2,1,0:T(8,128)(2,1)S(1)}, u32[]{:S(2)}, u32[]{:S(2)}) collective-permute-start(bf16[4,128,512]{2,1,0:T(8,128)(2,1)S(1)} %shard_map.80.own), channel_id=1, source_target_pairs={{0,6},{1,97},{2,0},{3,99},{4,2},{5,101},{6,4},{7,103},{8,14},{9,10... | collective-permute-start | bytes 1572872 | tf_op jit(solution)/shard_map/ppermute | solution.py:60
  34.5 3.8 %copy-done = bf16[4096,1187]{0,1:T(8,128)(2,1)S(1)} copy-done((bf16[4096,1187]{0,1:T(8,128)(2,1)S(1)}, bf16[4096,1187]{0,1:T(8,128)(2,1)}, u32[]{:S(2)}) %copy-start) | copy-done | bytes 9723928
  38.2 6.8 %shard_map.82 = (bf16[4,4,128,512]{3,2,1,0:T(8,128)(2,1)S(1)}, bf16[4,4,128,512]{3,2,1,0:T(8,128)(2,1)S(1)}) custom-call(bf16[512,1187]{1,0:T(8,128)(2,1)S(1)} %get-tuple-element.53.left_ref.hit_ref, bf16[1187,4096]{1,0:T(8,128)(2,1)S(1)} %bitcast.7), custom_call_target="tpu_custom_call" | custom-call | flops 1048576 | bytes 1024 | tf_op jit(solution)/shard_map/pallas_call | solution.py:359
  45.1 3.2 %shard_map.81.s_in = f32[512,1187]{1,0:T(8,128)S(1)} custom-call(bf16[4,128,512]{2,1,0:T(8,128)(2,1)S(1)} %shard_map.80.own, bf16[4,128,512]{2,1,0:T(8,128)(2,1)S(1)} %collective-permute-done.6.other, bf16[1187,4096]{1,0:T(8,128)(2,1)S(1)} %bitcast.8, f32[512,1187]{1,0:T(8,128)S(1)} %get-tuple-element.52.s_in), custom_call_target="tpu_custom_call", output_to_operand_aliasing={{}: (3, {})} | custom-call | flops 1048576 | bytes 1024 | tf_op jit(solution)/shard_map/pallas_call | solution.py:359
  49.7 2.8 %shard_map.83.s_in = f32[512,1187]{1,0:T(8,128)S(1)} custom-call(bf16[4,128,512]{2,1,0:T(8,128)(2,1)S(1)} %collective-permute-done.3.a1, bf16[4,128,512]{2,1,0:T(8,128)(2,1)S(1)} %collective-permute-done.4.a2, bf16[4,128,512]{2,1,0:T(8,128)(2,1)S(1)} %collective-permute-done.5.a3, bf16[1187,4096]{1,0:T(8,128)(2,1)S(1)} %bitcast.9, ...), custom_call_target="tpu_custom_call", output_to_operand_aliasing={{}: (4, {})} | custom-call | flops 1048576 | bytes 1024 | tf_op jit(solution)/shard_map/pallas_call | solution.py:359
  52.6 4.7 %shard_map.84 = (f32[512,1187]{1,0:T(8,128)S(1)}, bf16[512,1187]{1,0:T(8,128)(2,1)S(1)}, f32[16,128]{1,0:T(8,128)S(1)}) custom-call(bf16[4,128,512]{2,1,0:T(8,128)(2,1)S(1)} %collective-permute-done.7.a1, bf16[4,128,512]{2,1,0:T(8,128)(2,1)S(1)} %collective-permute-done.8.a2, ...), custom_call_target="tpu_custom_call", output_to_operand_aliasing={{0}: (4, {})} | custom-call | tf_op jit(solution)/shard_map/pallas_call | solution.py:359
  59.7 1.8 %collective-permute-start.12 = (f32[16,128]{1,0:T(8,128)S(1)}, f32[16,128]{1,0:T(8,128)S(1)}, u32[]{:S(2)}, u32[]{:S(2)}) collective-permute-start(f32[16,128]{1,0:T(8,128)S(1)} %get-tuple-element.67.s0), channel_id=1, source_target_pairs={{0,4},{1,5},{2,6},{3,7},{4,0},{5,1},{6,2},{7,3},{8,12},{9,13},{10,... | collective-permute-start | bytes 24584 | tf_op jit(solution)/shard_map/ppermute | solution.py:60
  62.5 2.1 %shard_map.86 = (bf16[4,128,512]{2,1,0:T(8,128)(2,1)S(1)}, bf16[4,128,512]{2,1,0:T(8,128)(2,1)S(1)}) custom-call(bf16[512,1187]{1,0:T(8,128)(2,1)S(1)} %get-tuple-element.61.left_ref, bf16[1187,4096]{1,0:T(8,128)(2,1)S(1)} %bitcast.11), custom_call_target="tpu_custom_call" | custom-call | flops 1048576 | bytes 1024 | tf_op jit(solution)/shard_map/pallas_call | solution.py:359
  64.6 2.1 %shard_map.87 = (bf16[4,128,512]{2,1,0:T(8,128)(2,1)S(1)}, bf16[4,128,512]{2,1,0:T(8,128)(2,1)S(1)}) custom-call(bf16[512,1187]{1,0:T(8,128)(2,1)S(1)} %get-tuple-element.61.left_ref, bf16[1187,4096]{1,0:T(8,128)(2,1)S(1)} %bitcast.12), custom_call_target="tpu_custom_call" | custom-call | flops 1048576 | bytes 1024 | tf_op jit(solution)/shard_map/pallas_call | solution.py:359
  68.0 12.0 %all_to_all.16.st_ref = f32[16,16,128]{2,1,0:T(8,128)S(1)} all-to-all(f32[16,16,128]{2,1,0:T(8,128)S(1)} %shard_map.88), channel_id=1, replica_groups=mesh['dp'=16,'vocab'=8] {'dp'}, dimensions={0} | all-to-all | bytes 262144 | tf_op jit(solution)/shard_map/all_to_all | solution.py:431
  80.6 1.7 %shard_map.91 = (bf16[4,128,512]{2,1,0:T(8,128)(2,1)S(1)}, bf16[4,128,512]{2,1,0:T(8,128)(2,1)S(1)}) custom-call(bf16[512,1187]{1,0:T(8,128)(2,1)S(1)} %get-tuple-element.61.left_ref, bf16[1187,4096]{1,0:T(8,128)(2,1)S(1)} %bitcast.13, f32[512,128]{1,0:T(8,128)S(1)} %get-tuple-element.82.factor_ref, bf16[4,4,128,512]{3,2,1,0:T(8,128)(2,1)S(1)} %get-tuple-element.77.tk_ref, ...), custom_call_target="tpu_custom_call" | custom-call | flops 3221225472 | bytes 1024 | tf_op jit(solution)/shard_map/pallas_call | solution.py:359
  83.1 1.7 %shard_map.92 = (bf16[4,128,512]{2,1,0:T(8,128)(2,1)S(1)}, f32[4,128,512]{2,1,0:T(8,128)S(1)}) custom-call(bf16[512,1187]{1,0:T(8,128)(2,1)S(1)} %get-tuple-element.61.left_ref, bf16[1187,4096]{1,0:T(8,128)(2,1)S(1)} %bitcast.14, f32[512,128]{1,0:T(8,128)S(1)} %get-tuple-element.82.factor_ref, bf16[4,4,128,512]{3,2,1,0:T(8,128)(2,1)S(1)} %get-tuple-element.77.tk_ref, ...), custom_call_target="tpu_custom_call" | custom-call | flops 3221225472 | bytes 1024 | tf_op jit(solution)/shard_map/pallas_call | solution.py:359
  84.9 1.4 %collective-permute-start.20 = (bf16[4,128,512]{2,1,0:T(8,128)(2,1)S(1)}, bf16[4,128,512]{2,1,0:T(8,128)(2,1)S(1)}, u32[]{:S(2)}, u32[]{:S(2)}) collective-permute-start(bf16[4,128,512]{2,1,0:T(8,128)(2,1)S(1)} %get-tuple-element.86), channel_id=1, source_target_pairs={{0,4},{1,65},{2,6},{3,67},{4,0},{5,69},{6,2},{7,71},{8,12},{9,73},... | collective-permute-start | bytes 1572872 | tf_op jit(solution)/shard_map/ppermute | solution.py:60
  86.3 2.0 %collective-permute-start.21 = (bf16[4,128,512]{2,1,0:T(8,128)(2,1)S(1)}, bf16[4,128,512]{2,1,0:T(8,128)(2,1)S(1)}, u32[]{:S(2)}, u32[]{:S(2)}) collective-permute-start(bf16[4,128,512]{2,1,0:T(8,128)(2,1)S(1)} %get-tuple-element.87), channel_id=1, source_target_pairs={{0,6},{1,97},{2,0},{3,99},{4,2},{5,101},{6,4},{7,103},{8,14},{9,10... | collective-permute-start | bytes 1572872 | tf_op jit(solution)/shard_map/ppermute | solution.py:60
  88.2 9.1 %collective-permute-done.20.r2 = bf16[4,128,512]{2,1,0:T(8,128)(2,1)S(1)} collective-permute-done((bf16[4,128,512]{2,1,0:T(8,128)(2,1)S(1)}, bf16[4,128,512]{2,1,0:T(8,128)(2,1)S(1)}, u32[]{:S(2)}, u32[]{:S(2)}) %collective-permute-start.20) | collective-permute-done | bytes 524320 | tf_op jit(solution)/shard_map/ppermute | solution.py:60
  98.5 2.7 %collective-permute-done.21.r3 = bf16[4,128,512]{2,1,0:T(8,128)(2,1)S(1)} collective-permute-done((bf16[4,128,512]{2,1,0:T(8,128)(2,1)S(1)}, bf16[4,128,512]{2,1,0:T(8,128)(2,1)S(1)}, u32[]{:S(2)}, u32[]{:S(2)}) %collective-permute-start.21) | collective-permute-done | bytes 524320 | tf_op jit(solution)/shard_map/ppermute | solution.py:60
  101.9 2.1 %collective-permute-start.23 = (f32[128,512]{1,0:T(8,128)S(1)}, f32[128,512]{1,0:T(8,128)S(1)}, u32[]{:S(2)}, u32[]{:S(2)}) collective-permute-start(f32[128,512]{1,0:T(8,128)S(1)} %get-tuple-element.90), channel_id=1, source_target_pairs={{0,64},{1,5},{2,66},{3,7},{4,68},{5,1},{6,70},{7,3},{8,72},{9,13},... | collective-permute-start | bytes 786440 | tf_op jit(solution)/shard_map/ppermute | solution.py:60
  105.4 1.4 %shard_map.90 = (bf16[256,128]{1,0:T(8,128)(2,1)S(1)}, bf16[64,256]{1,0:T(8,128)(2,1)S(1)}, f32[64,128]{1,0:T(8,128)S(1)}) custom-call(f32[1,112]{1,0:T(1,128)S(1)} %add_bitcast_fusion.meta_ref, f32[1,512]{1,0:T(1,128)S(1)} %add.70.cot_ref), custom_call_target="tpu_custom_call" | custom-call | flops 1048576 | bytes 1024 | tf_op jit(solution)/shard_map/pallas_call | solution.py:359
  106.8 5.1 %collective-permute-done.22.r1 = f32[128,512]{1,0:T(8,128)S(1)} collective-permute-done((f32[128,512]{1,0:T(8,128)S(1)}, f32[128,512]{1,0:T(8,128)S(1)}, u32[]{:S(2)}, u32[]{:S(2)}) %collective-permute-start.22) | collective-permute-done | bytes 262176 | tf_op jit(solution)/shard_map/ppermute | solution.py:60
  113.0 13.2 %all_to_all.17 = bf16[16,16,512]{2,1,0:T(8,128)(2,1)S(1)} all-to-all(bf16[16,16,512]{2,1,0:T(8,128)(2,1)S(1)} %bitcast.17), channel_id=1, replica_groups=mesh['dp'=16,'vocab'=8] {'dp'}, dimensions={0} | all-to-all | bytes 524288 | tf_op jit(solution)/shard_map/all_to_all | solution.py:455
  (61 shorter events, 20.0 us)
Async XLA Ops:
  20.4 5.0 %collective-permute-start = (bf16[128,512]{1,0:T(8,128)(2,1)S(1)}, bf16[128,512]{1,0:T(8,128)(2,1)S(1)}, u32[]{:S(2)}, u32[]{:S(2)}) collective-permute-start(bf16[128,512]{1,0:T(8,128)(2,1)S(1)} %shard_map.78.a0), channel_id=1, source_target_pairs={{0,96},{1,7},{2,98},{3,1},{4,100},{5,3},{6,102},{7,5},{8,104},{9,1... | collective-permute-start | bytes 393224 | tf_op jit(solution)/shard_map/ppermute | solution.py:60
  21.8 6.6 %collective-permute-start.1 = (bf16[128,512]{1,0:T(8,128)(2,1)S(1)}, bf16[128,512]{1,0:T(8,128)(2,1)S(1)}, u32[]{:S(2)}, u32[]{:S(2)}) collective-permute-start(bf16[128,512]{1,0:T(8,128)(2,1)S(1)} %shard_map.78.a0), channel_id=1, source_target_pairs={{0,64},{1,5},{2,66},{3,7},{4,68},{5,1},{6,70},{7,3},{8,72},{9,13},... | collective-permute-start | bytes 393224 | tf_op jit(solution)/shard_map/ppermute | solution.py:60
  22.6 7.1 %collective-permute-start.2 = (bf16[128,512]{1,0:T(8,128)(2,1)S(1)}, bf16[128,512]{1,0:T(8,128)(2,1)S(1)}, u32[]{:S(2)}, u32[]{:S(2)}) collective-permute-start(bf16[128,512]{1,0:T(8,128)(2,1)S(1)} %shard_map.78.a0), channel_id=1, source_target_pairs={{0,32},{1,3},{2,34},{3,5},{4,36},{5,7},{6,38},{7,1},{8,40},{9,11},... | collective-permute-start | bytes 393224 | tf_op jit(solution)/shard_map/ppermute | solution.py:60
  29.7 15.4 %collective-permute-start.6 = (bf16[4,128,512]{2,1,0:T(8,128)(2,1)S(1)}, bf16[4,128,512]{2,1,0:T(8,128)(2,1)S(1)}, u32[]{:S(2)}, u32[]{:S(2)}) collective-permute-start(bf16[4,128,512]{2,1,0:T(8,128)(2,1)S(1)} %shard_map.80.own), channel_id=1, source_target_pairs={{0,1},{1,0},{2,3},{3,2},{4,5},{5,4},{6,7},{7,6},{8,9},{9,8},{10,11... | collective-permute-start | bytes 1572872 | tf_op jit(solution)/shard_map/ppermute | solution.py:60
  29.8 18.5 %collective-permute-start.3 = (bf16[4,128,512]{2,1,0:T(8,128)(2,1)S(1)}, bf16[4,128,512]{2,1,0:T(8,128)(2,1)S(1)}, u32[]{:S(2)}, u32[]{:S(2)}) collective-permute-start(bf16[4,128,512]{2,1,0:T(8,128)(2,1)S(1)} %shard_map.80.own), channel_id=1, source_target_pairs={{0,6},{1,97},{2,0},{3,99},{4,2},{5,101},{6,4},{7,103},{8,14},{9,10... | collective-permute-start | bytes 1572872 | tf_op jit(solution)/shard_map/ppermute | solution.py:60
  32.9 15.4 %collective-permute-start.4 = (bf16[4,128,512]{2,1,0:T(8,128)(2,1)S(1)}, bf16[4,128,512]{2,1,0:T(8,128)(2,1)S(1)}, u32[]{:S(2)}, u32[]{:S(2)}) collective-permute-start(bf16[4,128,512]{2,1,0:T(8,128)(2,1)S(1)} %shard_map.80.own), channel_id=1, source_target_pairs={{0,4},{1,65},{2,6},{3,67},{4,0},{5,69},{6,2},{7,71},{8,12},{9,73},... | collective-permute-start | bytes 1572872 | tf_op jit(solution)/shard_map/ppermute | solution.py:60
  33.5 15.7 %collective-permute-start.5 = (bf16[4,128,512]{2,1,0:T(8,128)(2,1)S(1)}, bf16[4,128,512]{2,1,0:T(8,128)(2,1)S(1)}, u32[]{:S(2)}, u32[]{:S(2)}) collective-permute-start(bf16[4,128,512]{2,1,0:T(8,128)(2,1)S(1)} %shard_map.80.own), channel_id=1, source_target_pairs={{0,2},{1,33},{2,4},{3,35},{4,6},{5,37},{6,0},{7,39},{8,10},{9,41},... | collective-permute-start | bytes 1572872 | tf_op jit(solution)/shard_map/ppermute | solution.py:60
  49.2 3.3 %collective-permute-start.7 = (bf16[4,128,512]{2,1,0:T(8,128)(2,1)S(1)}, bf16[4,128,512]{2,1,0:T(8,128)(2,1)S(1)}, u32[]{:S(2)}, u32[]{:S(2)}) collective-permute-start(bf16[4,128,512]{2,1,0:T(8,128)(2,1)S(1)} %collective-permute-done.3.a1), channel_id=1, source_target_pairs={{0,1},{1,0},{2,3},{3,2},{4,5},{5,4},{6,7},{7,6},{8,9},{9,8},{10,11... | collective-permute-start | bytes 1572872 | tf_op jit(solution)/shard_map/ppermute | solution.py:60
  49.2 3.3 %collective-permute-start.8 = (bf16[4,128,512]{2,1,0:T(8,128)(2,1)S(1)}, bf16[4,128,512]{2,1,0:T(8,128)(2,1)S(1)}, u32[]{:S(2)}, u32[]{:S(2)}) collective-permute-start(bf16[4,128,512]{2,1,0:T(8,128)(2,1)S(1)} %collective-permute-done.4.a2), channel_id=1, source_target_pairs={{0,1},{1,0},{2,3},{3,2},{4,5},{5,4},{6,7},{7,6},{8,9},{9,8},{10,11... | collective-permute-start | bytes 1572872 | tf_op jit(solution)/shard_map/ppermute | solution.py:60
  49.7 2.9 %collective-permute-start.9 = (bf16[4,128,512]{2,1,0:T(8,128)(2,1)S(1)}, bf16[4,128,512]{2,1,0:T(8,128)(2,1)S(1)}, u32[]{:S(2)}, u32[]{:S(2)}) collective-permute-start(bf16[4,128,512]{2,1,0:T(8,128)(2,1)S(1)} %collective-permute-done.5.a3), channel_id=1, source_target_pairs={{0,1},{1,0},{2,3},{3,2},{4,5},{5,4},{6,7},{7,6},{8,9},{9,8},{10,11... | collective-permute-start | bytes 1572872 | tf_op jit(solution)/shard_map/ppermute | solution.py:60
  58.5 8.2 %collective-permute-start.11 = (f32[16,128]{1,0:T(8,128)S(1)}, f32[16,128]{1,0:T(8,128)S(1)}, u32[]{:S(2)}, u32[]{:S(2)}) collective-permute-start(f32[16,128]{1,0:T(8,128)S(1)} %get-tuple-element.67.s0), channel_id=1, source_target_pairs={{0,2},{1,3},{2,4},{3,5},{4,6},{5,7},{6,0},{7,1},{8,10},{9,11},{10,... | collective-permute-start | bytes 24584 | tf_op jit(solution)/shard_map/ppermute | solution.py:60
  59.7 7.0 %collective-permute-start.12 = (f32[16,128]{1,0:T(8,128)S(1)}, f32[16,128]{1,0:T(8,128)S(1)}, u32[]{:S(2)}, u32[]{:S(2)}) collective-permute-start(f32[16,128]{1,0:T(8,128)S(1)} %get-tuple-element.67.s0), channel_id=1, source_target_pairs={{0,4},{1,5},{2,6},{3,7},{4,0},{5,1},{6,2},{7,3},{8,12},{9,13},{10,... | collective-permute-start | bytes 24584 | tf_op jit(solution)/shard_map/ppermute | solution.py:60
  61.6 5.1 %collective-permute-start.13 = (f32[16,128]{1,0:T(8,128)S(1)}, f32[16,128]{1,0:T(8,128)S(1)}, u32[]{:S(2)}, u32[]{:S(2)}) collective-permute-start(f32[16,128]{1,0:T(8,128)S(1)} %get-tuple-element.67.s0), channel_id=1, source_target_pairs={{0,6},{1,7},{2,0},{3,1},{4,2},{5,3},{6,4},{7,5},{8,14},{9,15},{10,... | collective-permute-start | bytes 24584 | tf_op jit(solution)/shard_map/ppermute | solution.py:60
  66.7 13.9 %collective-permute-start.14 = (bf16[4,4,128,512]{3,2,1,0:T(8,128)(2,1)S(1)}, bf16[4,4,128,512]{3,2,1,0:T(8,128)(2,1)S(1)}, u32[]{:S(2)}, u32[]{:S(2)}) collective-permute-start(bf16[4,4,128,512]{3,2,1,0:T(8,128)(2,1)S(1)} %get-tuple-element.78), channel_id=1, source_target_pairs={{0,1},{1,0},{2,3},{3,2},{4,5},{5,4},{6,7},{7,6},{8,9},{9,8},{10,11... | collective-permute-start | bytes 6291464 | tf_op jit(solution)/shard_map/ppermute | solution.py:60
  66.8 13.8 %collective-permute-start.15 = (bf16[4,128,512]{2,1,0:T(8,128)(2,1)S(1)}, bf16[4,128,512]{2,1,0:T(8,128)(2,1)S(1)}, u32[]{:S(2)}, u32[]{:S(2)}) collective-permute-start(bf16[4,128,512]{2,1,0:T(8,128)(2,1)S(1)} %get-tuple-element.79), channel_id=1, source_target_pairs={{0,1},{1,0},{2,3},{3,2},{4,5},{5,4},{6,7},{7,6},{8,9},{9,8},{10,11... | collective-permute-start | bytes 1572872 | tf_op jit(solution)/shard_map/ppermute | solution.py:60
  67.3 13.3 %collective-permute-start.16 = (bf16[4,128,512]{2,1,0:T(8,128)(2,1)S(1)}, bf16[4,128,512]{2,1,0:T(8,128)(2,1)S(1)}, u32[]{:S(2)}, u32[]{:S(2)}) collective-permute-start(bf16[4,128,512]{2,1,0:T(8,128)(2,1)S(1)} %get-tuple-element.80), channel_id=1, source_target_pairs={{0,1},{1,0},{2,3},{3,2},{4,5},{5,4},{6,7},{7,6},{8,9},{9,8},{10,11... | collective-permute-start | bytes 1572872 | tf_op jit(solution)/shard_map/ppermute | solution.py:60
  67.4 15.7 %collective-permute-start.17 = (bf16[4,128,512]{2,1,0:T(8,128)(2,1)S(1)}, bf16[4,128,512]{2,1,0:T(8,128)(2,1)S(1)}, u32[]{:S(2)}, u32[]{:S(2)}) collective-permute-start(bf16[4,128,512]{2,1,0:T(8,128)(2,1)S(1)} %get-tuple-element.83), channel_id=1, source_target_pairs={{0,1},{1,0},{2,3},{3,2},{4,5},{5,4},{6,7},{7,6},{8,9},{9,8},{10,11... | collective-permute-start | bytes 1572872 | tf_op jit(solution)/shard_map/ppermute | solution.py:60
  67.8 15.3 %collective-permute-start.18 = (bf16[4,128,512]{2,1,0:T(8,128)(2,1)S(1)}, bf16[4,128,512]{2,1,0:T(8,128)(2,1)S(1)}, u32[]{:S(2)}, u32[]{:S(2)}) collective-permute-start(bf16[4,128,512]{2,1,0:T(8,128)(2,1)S(1)} %get-tuple-element.84), channel_id=1, source_target_pairs={{0,1},{1,0},{2,3},{3,2},{4,5},{5,4},{6,7},{7,6},{8,9},{9,8},{10,11... | collective-permute-start | bytes 1572872 | tf_op jit(solution)/shard_map/ppermute | solution.py:60
  82.4 16.1 %collective-permute-start.19 = (bf16[4,128,512]{2,1,0:T(8,128)(2,1)S(1)}, bf16[4,128,512]{2,1,0:T(8,128)(2,1)S(1)}, u32[]{:S(2)}, u32[]{:S(2)}) collective-permute-start(bf16[4,128,512]{2,1,0:T(8,128)(2,1)S(1)} %get-tuple-element.81), channel_id=1, source_target_pairs={{0,2},{1,33},{2,4},{3,35},{4,6},{5,37},{6,0},{7,39},{8,10},{9,41},... | collective-permute-start | bytes 1572872 | tf_op jit(solution)/shard_map/ppermute | solution.py:60
  84.9 12.4 %collective-permute-start.20 = (bf16[4,128,512]{2,1,0:T(8,128)(2,1)S(1)}, bf16[4,128,512]{2,1,0:T(8,128)(2,1)S(1)}, u32[]{:S(2)}, u32[]{:S(2)}) collective-permute-start(bf16[4,128,512]{2,1,0:T(8,128)(2,1)S(1)} %get-tuple-element.86), channel_id=1, source_target_pairs={{0,4},{1,65},{2,6},{3,67},{4,0},{5,69},{6,2},{7,71},{8,12},{9,73},... | collective-permute-start | bytes 1572872 | tf_op jit(solution)/shard_map/ppermute | solution.py:60
  86.3 14.9 %collective-permute-start.21 = (bf16[4,128,512]{2,1,0:T(8,128)(2,1)S(1)}, bf16[4,128,512]{2,1,0:T(8,128)(2,1)S(1)}, u32[]{:S(2)}, u32[]{:S(2)}) collective-permute-start(bf16[4,128,512]{2,1,0:T(8,128)(2,1)S(1)} %get-tuple-element.87), channel_id=1, source_target_pairs={{0,6},{1,97},{2,0},{3,99},{4,2},{5,101},{6,4},{7,103},{8,14},{9,10... | collective-permute-start | bytes 1572872 | tf_op jit(solution)/shard_map/ppermute | solution.py:60
  101.4 10.5 %collective-permute-start.22 = (f32[128,512]{1,0:T(8,128)S(1)}, f32[128,512]{1,0:T(8,128)S(1)}, u32[]{:S(2)}, u32[]{:S(2)}) collective-permute-start(f32[128,512]{1,0:T(8,128)S(1)} %get-tuple-element.89), channel_id=1, source_target_pairs={{0,32},{1,3},{2,34},{3,5},{4,36},{5,7},{6,38},{7,1},{8,40},{9,11},... | collective-permute-start | bytes 786440 | tf_op jit(solution)/shard_map/ppermute | solution.py:60
  101.9 10.0 %collective-permute-start.23 = (f32[128,512]{1,0:T(8,128)S(1)}, f32[128,512]{1,0:T(8,128)S(1)}, u32[]{:S(2)}, u32[]{:S(2)}) collective-permute-start(f32[128,512]{1,0:T(8,128)S(1)} %get-tuple-element.90), channel_id=1, source_target_pairs={{0,64},{1,5},{2,66},{3,7},{4,68},{5,1},{6,70},{7,3},{8,72},{9,13},... | collective-permute-start | bytes 786440 | tf_op jit(solution)/shard_map/ppermute | solution.py:60
  104.0 8.7 %collective-permute-start.24 = (f32[128,512]{1,0:T(8,128)S(1)}, f32[128,512]{1,0:T(8,128)S(1)}, u32[]{:S(2)}, u32[]{:S(2)}) collective-permute-start(f32[128,512]{1,0:T(8,128)S(1)} %get-tuple-element.91), channel_id=1, source_target_pairs={{0,96},{1,7},{2,98},{3,1},{4,100},{5,3},{6,102},{7,5},{8,104},{9,1... | collective-permute-start | bytes 786440 | tf_op jit(solution)/shard_map/ppermute | solution.py:60
  (4 other events, 12.7 us)

commit v2 on v1

--- a/solution.py
+++ b/solution.py
@@ -426,14 +426,14 @@
         send.update(zip(ds, out))
     line, send, target_send = lax.optimization_barrier((line, send, target_send))
     stats = call(line_kernel, line, sds((N_DP, 16, 128), F32))
-    got = {d: permute(send[d], CORE_PERM) for d in (1, 3, 2, 0)}
+    got = {d: permute(send[d], CORE_PERM) for d in (2, 1, 3, 0)}
     target_got = permute(target_send, CORE_PERM)
     stats = lax.all_to_all(stats, "dp", 0, 0, tiled=True)
     factors, logprobs = call(
         factor_kernel, (stats, chip), [sds((512, 128), F32), sds((1, 32), F32)], scratch=[pltpu.VMEM((8, 128), F32)],
     )
     ring = {}
-    for ds in pairs:
+    for ds in ((2, 1), (3, 0)):
         out = call(
             functools.partial(combine_kernel, ds),
             (exps, head, factors, target_keep, target_got, *[got[d] for d in ds]),

time: 127 us -> 127 us (level)
  transfers between devices with their start and end apart: 25 -> 25, of which waited for: 11 -> 10; matrix products, arithmetic and copies ran while one was open for 0% -> 0% of each run, Pallas kernels for 19% -> 18%
where the time goes in v2:
time: 127 us
  blocking collectives  42.7 us (34%)
  Pallas kernels  30.8 us (24%)
  waiting for transfers between devices  25.8 us (20%)
  starting transfers between devices  20.9 us (16%)
  local copies, waits for them, and re-layouts  4.86 us (4%)
    pallas_call x19, Pallas kernels, call(): pl.pallas_call(kernel, out_shape=outs, in_specs=in_specs or [VM] * len(in...  30.8 us
    ppermute x25, waiting for transfers between devices, permute(): return lax.ppermute(v, ('dp', 'vocab'), pairs)  25.8 us
    ppermute x25, starting transfers between devices, permute(): return lax.ppermute(v, ('dp', 'vocab'), pairs)  20.9 us
    all_to_all x1, blocking collectives, per_device(): arrived = lax.all_to_all(outgoing, 'dp', 0, 0, tiled=True)  17.6 us
    all_to_all x1, blocking collectives, per_device(): lax.all_to_all(returning.reshape(N_DP, 16, FEAT), 'dp', 0, 0, tiled=True)  13.1 us
    all_to_all x1, blocking collectives, per_device(): stats = lax.all_to_all(stats, 'dp', 0, 0, tiled=True)  12 us
    unnamed x6, local copies, waits for them, and re-layouts  4.62 us
  transfers between devices with their start and end apart: 25, of which 10 were waited for; matrix products, arithmetic and copies ran while one was open for 0% of the time, Pallas kernels for 18%

profile of v2, /device:TPU:0, one launch (start us, length us, event | category | flops | bytes accessed | tf_op | source)
XLA Modules:
  0.0 126.7 jit_solution(12306790726129716119)
XLA Ops:
  2.5 17.6 %all_to_all.15 = bf16[16,24,512]{2,1,0:T(8,128)(2,1)S(1)} all-to-all(bf16[16,24,512]{2,1,0:T(8,128)(2,1)S(1)} %shard_map.77), channel_id=1, replica_groups=mesh['dp'=16,'vocab'=8] {'dp'}, dimensions={0} | all-to-all | bytes 786432 | tf_op jit(solution)/shard_map/all_to_all | solution.py:382
  20.4 1.4 %collective-permute-start = (bf16[128,512]{1,0:T(8,128)(2,1)S(1)}, bf16[128,512]{1,0:T(8,128)(2,1)S(1)}, u32[]{:S(2)}, u32[]{:S(2)}) collective-permute-start(bf16[128,512]{1,0:T(8,128)(2,1)S(1)} %shard_map.78.a0), channel_id=1, source_target_pairs={{0,96},{1,7},{2,98},{3,1},{4,100},{5,3},{6,102},{7,5},{8,104},{9,1... | collective-permute-start | bytes 393224 | tf_op jit(solution)/shard_map/ppermute | solution.py:60
  23.4 1.5 %shard_map.79 = (bf16[512,1187]{1,0:T(8,128)(2,1)S(1)}, f32[512,1187]{1,0:T(8,128)S(1)}) custom-call(s32[1,512]{1,0:T(1,128)S(1)} %convert_element_type.37.tok_ref, s32[1,512]{1,0:T(1,128)S(1)} %convert_element_type.39.seg_ref), custom_call_target="tpu_custom_call" | custom-call | flops 1048576 | bytes 1024 | tf_op jit(solution)/shard_map/pallas_call | solution.py:359
  25.4 2.9 %collective-permute-done.1.a2 = bf16[128,512]{1,0:T(8,128)(2,1)S(1)} collective-permute-done((bf16[128,512]{1,0:T(8,128)(2,1)S(1)}, bf16[128,512]{1,0:T(8,128)(2,1)S(1)}, u32[]{:S(2)}, u32[]{:S(2)}) %collective-permute-start.1) | collective-permute-done | bytes 131104 | tf_op jit(solution)/shard_map/ppermute | solution.py:60
  29.8 3.1 %collective-permute-start.3 = (bf16[4,128,512]{2,1,0:T(8,128)(2,1)S(1)}, bf16[4,128,512]{2,1,0:T(8,128)(2,1)S(1)}, u32[]{:S(2)}, u32[]{:S(2)}) collective-permute-start(bf16[4,128,512]{2,1,0:T(8,128)(2,1)S(1)} %shard_map.80.own), channel_id=1, source_target_pairs={{0,6},{1,97},{2,0},{3,99},{4,2},{5,101},{6,4},{7,103},{8,14},{9,10... | collective-permute-start | bytes 1572872 | tf_op jit(solution)/shard_map/ppermute | solution.py:60
  34.5 3.8 %copy-done = bf16[4096,1187]{0,1:T(8,128)(2,1)S(1)} copy-done((bf16[4096,1187]{0,1:T(8,128)(2,1)S(1)}, bf16[4096,1187]{0,1:T(8,128)(2,1)}, u32[]{:S(2)}) %copy-start) | copy-done | bytes 9723928
  38.2 6.8 %shard_map.82 = (bf16[4,4,128,512]{3,2,1,0:T(8,128)(2,1)S(1)}, bf16[4,4,128,512]{3,2,1,0:T(8,128)(2,1)S(1)}) custom-call(bf16[512,1187]{1,0:T(8,128)(2,1)S(1)} %get-tuple-element.53.left_ref.hit_ref, bf16[1187,4096]{1,0:T(8,128)(2,1)S(1)} %bitcast.7), custom_call_target="tpu_custom_call" | custom-call | flops 1048576 | bytes 1024 | tf_op jit(solution)/shard_map/pallas_call | solution.py:359
  45.1 3.2 %shard_map.81.s_in = f32[512,1187]{1,0:T(8,128)S(1)} custom-call(bf16[4,128,512]{2,1,0:T(8,128)(2,1)S(1)} %shard_map.80.own, bf16[4,128,512]{2,1,0:T(8,128)(2,1)S(1)} %collective-permute-done.6.other, bf16[1187,4096]{1,0:T(8,128)(2,1)S(1)} %bitcast.8, f32[512,1187]{1,0:T(8,128)S(1)} %get-tuple-element.52.s_in), custom_call_target="tpu_custom_call", output_to_operand_aliasing={{}: (3, {})} | custom-call | flops 1048576 | bytes 1024 | tf_op jit(solution)/shard_map/pallas_call | solution.py:359
  49.7 2.8 %shard_map.83.s_in = f32[512,1187]{1,0:T(8,128)S(1)} custom-call(bf16[4,128,512]{2,1,0:T(8,128)(2,1)S(1)} %collective-permute-done.3.a1, bf16[4,128,512]{2,1,0:T(8,128)(2,1)S(1)} %collective-permute-done.4.a2, bf16[4,128,512]{2,1,0:T(8,128)(2,1)S(1)} %collective-permute-done.5.a3, bf16[1187,4096]{1,0:T(8,128)(2,1)S(1)} %bitcast.9, ...), custom_call_target="tpu_custom_call", output_to_operand_aliasing={{}: (4, {})} | custom-call | flops 1048576 | bytes 1024 | tf_op jit(solution)/shard_map/pallas_call | solution.py:359
  52.6 4.7 %shard_map.84 = (f32[512,1187]{1,0:T(8,128)S(1)}, bf16[512,1187]{1,0:T(8,128)(2,1)S(1)}, f32[16,128]{1,0:T(8,128)S(1)}) custom-call(bf16[4,128,512]{2,1,0:T(8,128)(2,1)S(1)} %collective-permute-done.7.a1, bf16[4,128,512]{2,1,0:T(8,128)(2,1)S(1)} %collective-permute-done.8.a2, ...), custom_call_target="tpu_custom_call", output_to_operand_aliasing={{0}: (4, {})} | custom-call | tf_op jit(solution)/shard_map/pallas_call | solution.py:359
  59.7 1.8 %collective-permute-start.12 = (f32[16,128]{1,0:T(8,128)S(1)}, f32[16,128]{1,0:T(8,128)S(1)}, u32[]{:S(2)}, u32[]{:S(2)}) collective-permute-start(f32[16,128]{1,0:T(8,128)S(1)} %get-tuple-element.67.s0), channel_id=1, source_target_pairs={{0,4},{1,5},{2,6},{3,7},{4,0},{5,1},{6,2},{7,3},{8,12},{9,13},{10,... | collective-permute-start | bytes 24584 | tf_op jit(solution)/shard_map/ppermute | solution.py:60
  62.5 2.1 %shard_map.86 = (bf16[4,128,512]{2,1,0:T(8,128)(2,1)S(1)}, bf16[4,128,512]{2,1,0:T(8,128)(2,1)S(1)}) custom-call(bf16[512,1187]{1,0:T(8,128)(2,1)S(1)} %get-tuple-element.61.left_ref, bf16[1187,4096]{1,0:T(8,128)(2,1)S(1)} %bitcast.11), custom_call_target="tpu_custom_call" | custom-call | flops 1048576 | bytes 1024 | tf_op jit(solution)/shard_map/pallas_call | solution.py:359
  64.6 2.1 %shard_map.87 = (bf16[4,128,512]{2,1,0:T(8,128)(2,1)S(1)}, bf16[4,128,512]{2,1,0:T(8,128)(2,1)S(1)}) custom-call(bf16[512,1187]{1,0:T(8,128)(2,1)S(1)} %get-tuple-element.61.left_ref, bf16[1187,4096]{1,0:T(8,128)(2,1)S(1)} %bitcast.12), custom_call_target="tpu_custom_call" | custom-call | flops 1048576 | bytes 1024 | tf_op jit(solution)/shard_map/pallas_call | solution.py:359
  68.0 12.0 %all_to_all.16.st_ref = f32[16,16,128]{2,1,0:T(8,128)S(1)} all-to-all(f32[16,16,128]{2,1,0:T(8,128)S(1)} %shard_map.88), channel_id=1, replica_groups=mesh['dp'=16,'vocab'=8] {'dp'}, dimensions={0} | all-to-all | bytes 262144 | tf_op jit(solution)/shard_map/all_to_all | solution.py:431
  80.6 1.7 %shard_map.91 = (bf16[4,128,512]{2,1,0:T(8,128)(2,1)S(1)}, bf16[4,128,512]{2,1,0:T(8,128)(2,1)S(1)}) custom-call(bf16[512,1187]{1,0:T(8,128)(2,1)S(1)} %get-tuple-element.61.left_ref, bf16[1187,4096]{1,0:T(8,128)(2,1)S(1)} %bitcast.13, f32[512,128]{1,0:T(8,128)S(1)} %get-tuple-element.82.factor_ref, bf16[4,4,128,512]{3,2,1,0:T(8,128)(2,1)S(1)} %get-tuple-element.77.tk_ref, ...), custom_call_target="tpu_custom_call" | custom-call | flops 3221225472 | bytes 1024 | tf_op jit(solution)/shard_map/pallas_call | solution.py:359
  82.4 2.0 %shard_map.92 = (bf16[4,128,512]{2,1,0:T(8,128)(2,1)S(1)}, f32[4,128,512]{2,1,0:T(8,128)S(1)}) custom-call(bf16[512,1187]{1,0:T(8,128)(2,1)S(1)} %get-tuple-element.61.left_ref, bf16[1187,4096]{1,0:T(8,128)(2,1)S(1)} %bitcast.14, f32[512,128]{1,0:T(8,128)S(1)} %get-tuple-element.82.factor_ref, bf16[4,4,128,512]{3,2,1,0:T(8,128)(2,1)S(1)} %get-tuple-element.77.tk_ref, ...), custom_call_target="tpu_custom_call" | custom-call | flops 3221225472 | bytes 1024 | tf_op jit(solution)/shard_map/pallas_call | solution.py:359
  85.0 1.5 %collective-permute-start.19 = (bf16[4,128,512]{2,1,0:T(8,128)(2,1)S(1)}, bf16[4,128,512]{2,1,0:T(8,128)(2,1)S(1)}, u32[]{:S(2)}, u32[]{:S(2)}) collective-permute-start(bf16[4,128,512]{2,1,0:T(8,128)(2,1)S(1)} %get-tuple-element.86), channel_id=1, source_target_pairs={{0,2},{1,33},{2,4},{3,35},{4,6},{5,37},{6,0},{7,39},{8,10},{9,41},... | collective-permute-start | bytes 1572872 | tf_op jit(solution)/shard_map/ppermute | solution.py:60
  86.5 1.3 %collective-permute-start.20 = (bf16[4,128,512]{2,1,0:T(8,128)(2,1)S(1)}, bf16[4,128,512]{2,1,0:T(8,128)(2,1)S(1)}, u32[]{:S(2)}, u32[]{:S(2)}) collective-permute-start(bf16[4,128,512]{2,1,0:T(8,128)(2,1)S(1)} %get-tuple-element.81), channel_id=1, source_target_pairs={{0,4},{1,65},{2,6},{3,67},{4,0},{5,69},{6,2},{7,71},{8,12},{9,73},... | collective-permute-start | bytes 1572872 | tf_op jit(solution)/shard_map/ppermute | solution.py:60
  87.8 5.8 %collective-permute-done.21.r3 = bf16[4,128,512]{2,1,0:T(8,128)(2,1)S(1)} collective-permute-done((bf16[4,128,512]{2,1,0:T(8,128)(2,1)S(1)}, bf16[4,128,512]{2,1,0:T(8,128)(2,1)S(1)}, u32[]{:S(2)}, u32[]{:S(2)}) %collective-permute-start.21) | collective-permute-done | bytes 524320 | tf_op jit(solution)/shard_map/ppermute | solution.py:60
  93.6 7.3 %collective-permute-done.19.r1 = bf16[4,128,512]{2,1,0:T(8,128)(2,1)S(1)} collective-permute-done((bf16[4,128,512]{2,1,0:T(8,128)(2,1)S(1)}, bf16[4,128,512]{2,1,0:T(8,128)(2,1)S(1)}, u32[]{:S(2)}, u32[]{:S(2)}) %collective-permute-start.19) | collective-permute-done | bytes 524320 | tf_op jit(solution)/shard_map/ppermute | solution.py:60
  101.6 2.2 %collective-permute-start.23 = (f32[128,512]{1,0:T(8,128)S(1)}, f32[128,512]{1,0:T(8,128)S(1)}, u32[]{:S(2)}, u32[]{:S(2)}) collective-permute-start(f32[128,512]{1,0:T(8,128)S(1)} %get-tuple-element.90), channel_id=1, source_target_pairs={{0,64},{1,5},{2,66},{3,7},{4,68},{5,1},{6,70},{7,3},{8,72},{9,13},... | collective-permute-start | bytes 786440 | tf_op jit(solution)/shard_map/ppermute | solution.py:60
  105.1 1.4 %shard_map.90 = (bf16[256,128]{1,0:T(8,128)(2,1)S(1)}, bf16[64,256]{1,0:T(8,128)(2,1)S(1)}, f32[64,128]{1,0:T(8,128)S(1)}) custom-call(f32[1,112]{1,0:T(1,128)S(1)} %add_bitcast_fusion.meta_ref, f32[1,512]{1,0:T(1,128)S(1)} %add.70.cot_ref), custom_call_target="tpu_custom_call" | custom-call | flops 1048576 | bytes 1024 | tf_op jit(solution)/shard_map/pallas_call | solution.py:359
  106.5 5.1 %collective-permute-done.22.r1 = f32[128,512]{1,0:T(8,128)S(1)} collective-permute-done((f32[128,512]{1,0:T(8,128)S(1)}, f32[128,512]{1,0:T(8,128)S(1)}, u32[]{:S(2)}, u32[]{:S(2)}) %collective-permute-start.22) | collective-permute-done | bytes 262176 | tf_op jit(solution)/shard_map/ppermute | solution.py:60
  112.8 13.1 %all_to_all.17 = bf16[16,16,512]{2,1,0:T(8,128)(2,1)S(1)} all-to-all(bf16[16,16,512]{2,1,0:T(8,128)(2,1)S(1)} %bitcast.17), channel_id=1, replica_groups=mesh['dp'=16,'vocab'=8] {'dp'}, dimensions={0} | all-to-all | bytes 524288 | tf_op jit(solution)/shard_map/all_to_all | solution.py:455
  (61 shorter events, 18.6 us)
Async XLA Ops:
  20.4 5.0 %collective-permute-start = (bf16[128,512]{1,0:T(8,128)(2,1)S(1)}, bf16[128,512]{1,0:T(8,128)(2,1)S(1)}, u32[]{:S(2)}, u32[]{:S(2)}) collective-permute-start(bf16[128,512]{1,0:T(8,128)(2,1)S(1)} %shard_map.78.a0), channel_id=1, source_target_pairs={{0,96},{1,7},{2,98},{3,1},{4,100},{5,3},{6,102},{7,5},{8,104},{9,1... | collective-permute-start | bytes 393224 | tf_op jit(solution)/shard_map/ppermute | solution.py:60
  21.8 6.6 %collective-permute-start.1 = (bf16[128,512]{1,0:T(8,128)(2,1)S(1)}, bf16[128,512]{1,0:T(8,128)(2,1)S(1)}, u32[]{:S(2)}, u32[]{:S(2)}) collective-permute-start(bf16[128,512]{1,0:T(8,128)(2,1)S(1)} %shard_map.78.a0), channel_id=1, source_target_pairs={{0,64},{1,5},{2,66},{3,7},{4,68},{5,1},{6,70},{7,3},{8,72},{9,13},... | collective-permute-start | bytes 393224 | tf_op jit(solution)/shard_map/ppermute | solution.py:60
  22.6 7.1 %collective-permute-start.2 = (bf16[128,512]{1,0:T(8,128)(2,1)S(1)}, bf16[128,512]{1,0:T(8,128)(2,1)S(1)}, u32[]{:S(2)}, u32[]{:S(2)}) collective-permute-start(bf16[128,512]{1,0:T(8,128)(2,1)S(1)} %shard_map.78.a0), channel_id=1, source_target_pairs={{0,32},{1,3},{2,34},{3,5},{4,36},{5,7},{6,38},{7,1},{8,40},{9,11},... | collective-permute-start | bytes 393224 | tf_op jit(solution)/shard_map/ppermute | solution.py:60
  29.7 15.4 %collective-permute-start.6 = (bf16[4,128,512]{2,1,0:T(8,128)(2,1)S(1)}, bf16[4,128,512]{2,1,0:T(8,128)(2,1)S(1)}, u32[]{:S(2)}, u32[]{:S(2)}) collective-permute-start(bf16[4,128,512]{2,1,0:T(8,128)(2,1)S(1)} %shard_map.80.own), channel_id=1, source_target_pairs={{0,1},{1,0},{2,3},{3,2},{4,5},{5,4},{6,7},{7,6},{8,9},{9,8},{10,11... | collective-permute-start | bytes 1572872 | tf_op jit(solution)/shard_map/ppermute | solution.py:60
  29.8 18.5 %collective-permute-start.3 = (bf16[4,128,512]{2,1,0:T(8,128)(2,1)S(1)}, bf16[4,128,512]{2,1,0:T(8,128)(2,1)S(1)}, u32[]{:S(2)}, u32[]{:S(2)}) collective-permute-start(bf16[4,128,512]{2,1,0:T(8,128)(2,1)S(1)} %shard_map.80.own), channel_id=1, source_target_pairs={{0,6},{1,97},{2,0},{3,99},{4,2},{5,101},{6,4},{7,103},{8,14},{9,10... | collective-permute-start | bytes 1572872 | tf_op jit(solution)/shard_map/ppermute | solution.py:60
  32.9 15.4 %collective-permute-start.4 = (bf16[4,128,512]{2,1,0:T(8,128)(2,1)S(1)}, bf16[4,128,512]{2,1,0:T(8,128)(2,1)S(1)}, u32[]{:S(2)}, u32[]{:S(2)}) collective-permute-start(bf16[4,128,512]{2,1,0:T(8,128)(2,1)S(1)} %shard_map.80.own), channel_id=1, source_target_pairs={{0,4},{1,65},{2,6},{3,67},{4,0},{5,69},{6,2},{7,71},{8,12},{9,73},... | collective-permute-start | bytes 1572872 | tf_op jit(solution)/shard_map/ppermute | solution.py:60
  33.5 15.7 %collective-permute-start.5 = (bf16[4,128,512]{2,1,0:T(8,128)(2,1)S(1)}, bf16[4,128,512]{2,1,0:T(8,128)(2,1)S(1)}, u32[]{:S(2)}, u32[]{:S(2)}) collective-permute-start(bf16[4,128,512]{2,1,0:T(8,128)(2,1)S(1)} %shard_map.80.own), channel_id=1, source_target_pairs={{0,2},{1,33},{2,4},{3,35},{4,6},{5,37},{6,0},{7,39},{8,10},{9,41},... | collective-permute-start | bytes 1572872 | tf_op jit(solution)/shard_map/ppermute | solution.py:60
  49.2 3.3 %collective-permute-start.7 = (bf16[4,128,512]{2,1,0:T(8,128)(2,1)S(1)}, bf16[4,128,512]{2,1,0:T(8,128)(2,1)S(1)}, u32[]{:S(2)}, u32[]{:S(2)}) collective-permute-start(bf16[4,128,512]{2,1,0:T(8,128)(2,1)S(1)} %collective-permute-done.3.a1), channel_id=1, source_target_pairs={{0,1},{1,0},{2,3},{3,2},{4,5},{5,4},{6,7},{7,6},{8,9},{9,8},{10,11... | collective-permute-start | bytes 1572872 | tf_op jit(solution)/shard_map/ppermute | solution.py:60
  49.2 3.3 %collective-permute-start.8 = (bf16[4,128,512]{2,1,0:T(8,128)(2,1)S(1)}, bf16[4,128,512]{2,1,0:T(8,128)(2,1)S(1)}, u32[]{:S(2)}, u32[]{:S(2)}) collective-permute-start(bf16[4,128,512]{2,1,0:T(8,128)(2,1)S(1)} %collective-permute-done.4.a2), channel_id=1, source_target_pairs={{0,1},{1,0},{2,3},{3,2},{4,5},{5,4},{6,7},{7,6},{8,9},{9,8},{10,11... | collective-permute-start | bytes 1572872 | tf_op jit(solution)/shard_map/ppermute | solution.py:60
  49.7 2.9 %collective-permute-start.9 = (bf16[4,128,512]{2,1,0:T(8,128)(2,1)S(1)}, bf16[4,128,512]{2,1,0:T(8,128)(2,1)S(1)}, u32[]{:S(2)}, u32[]{:S(2)}) collective-permute-start(bf16[4,128,512]{2,1,0:T(8,128)(2,1)S(1)} %collective-permute-done.5.a3), channel_id=1, source_target_pairs={{0,1},{1,0},{2,3},{3,2},{4,5},{5,4},{6,7},{7,6},{8,9},{9,8},{10,11... | collective-permute-start | bytes 1572872 | tf_op jit(solution)/shard_map/ppermute | solution.py:60
  58.5 8.2 %collective-permute-start.11 = (f32[16,128]{1,0:T(8,128)S(1)}, f32[16,128]{1,0:T(8,128)S(1)}, u32[]{:S(2)}, u32[]{:S(2)}) collective-permute-start(f32[16,128]{1,0:T(8,128)S(1)} %get-tuple-element.67.s0), channel_id=1, source_target_pairs={{0,2},{1,3},{2,4},{3,5},{4,6},{5,7},{6,0},{7,1},{8,10},{9,11},{10,... | collective-permute-start | bytes 24584 | tf_op jit(solution)/shard_map/ppermute | solution.py:60
  59.7 7.0 %collective-permute-start.12 = (f32[16,128]{1,0:T(8,128)S(1)}, f32[16,128]{1,0:T(8,128)S(1)}, u32[]{:S(2)}, u32[]{:S(2)}) collective-permute-start(f32[16,128]{1,0:T(8,128)S(1)} %get-tuple-element.67.s0), channel_id=1, source_target_pairs={{0,4},{1,5},{2,6},{3,7},{4,0},{5,1},{6,2},{7,3},{8,12},{9,13},{10,... | collective-permute-start | bytes 24584 | tf_op jit(solution)/shard_map/ppermute | solution.py:60
  61.6 5.1 %collective-permute-start.13 = (f32[16,128]{1,0:T(8,128)S(1)}, f32[16,128]{1,0:T(8,128)S(1)}, u32[]{:S(2)}, u32[]{:S(2)}) collective-permute-start(f32[16,128]{1,0:T(8,128)S(1)} %get-tuple-element.67.s0), channel_id=1, source_target_pairs={{0,6},{1,7},{2,0},{3,1},{4,2},{5,3},{6,4},{7,5},{8,14},{9,15},{10,... | collective-permute-start | bytes 24584 | tf_op jit(solution)/shard_map/ppermute | solution.py:60
  66.7 13.9 %collective-permute-start.14 = (bf16[4,4,128,512]{3,2,1,0:T(8,128)(2,1)S(1)}, bf16[4,4,128,512]{3,2,1,0:T(8,128)(2,1)S(1)}, u32[]{:S(2)}, u32[]{:S(2)}) collective-permute-start(bf16[4,4,128,512]{3,2,1,0:T(8,128)(2,1)S(1)} %get-tuple-element.78), channel_id=1, source_target_pairs={{0,1},{1,0},{2,3},{3,2},{4,5},{5,4},{6,7},{7,6},{8,9},{9,8},{10,11... | collective-permute-start | bytes 6291464 | tf_op jit(solution)/shard_map/ppermute | solution.py:60
  66.8 13.8 %collective-permute-start.15 = (bf16[4,128,512]{2,1,0:T(8,128)(2,1)S(1)}, bf16[4,128,512]{2,1,0:T(8,128)(2,1)S(1)}, u32[]{:S(2)}, u32[]{:S(2)}) collective-permute-start(bf16[4,128,512]{2,1,0:T(8,128)(2,1)S(1)} %get-tuple-element.79), channel_id=1, source_target_pairs={{0,1},{1,0},{2,3},{3,2},{4,5},{5,4},{6,7},{7,6},{8,9},{9,8},{10,11... | collective-permute-start | bytes 1572872 | tf_op jit(solution)/shard_map/ppermute | solution.py:60
  67.3 13.3 %collective-permute-start.16 = (bf16[4,128,512]{2,1,0:T(8,128)(2,1)S(1)}, bf16[4,128,512]{2,1,0:T(8,128)(2,1)S(1)}, u32[]{:S(2)}, u32[]{:S(2)}) collective-permute-start(bf16[4,128,512]{2,1,0:T(8,128)(2,1)S(1)} %get-tuple-element.80), channel_id=1, source_target_pairs={{0,1},{1,0},{2,3},{3,2},{4,5},{5,4},{6,7},{7,6},{8,9},{9,8},{10,11... | collective-permute-start | bytes 1572872 | tf_op jit(solution)/shard_map/ppermute | solution.py:60
  67.4 15.0 %collective-permute-start.17 = (bf16[4,128,512]{2,1,0:T(8,128)(2,1)S(1)}, bf16[4,128,512]{2,1,0:T(8,128)(2,1)S(1)}, u32[]{:S(2)}, u32[]{:S(2)}) collective-permute-start(bf16[4,128,512]{2,1,0:T(8,128)(2,1)S(1)} %get-tuple-element.83), channel_id=1, source_target_pairs={{0,1},{1,0},{2,3},{3,2},{4,5},{5,4},{6,7},{7,6},{8,9},{9,8},{10,11... | collective-permute-start | bytes 1572872 | tf_op jit(solution)/shard_map/ppermute | solution.py:60
  67.8 14.6 %collective-permute-start.18 = (bf16[4,128,512]{2,1,0:T(8,128)(2,1)S(1)}, bf16[4,128,512]{2,1,0:T(8,128)(2,1)S(1)}, u32[]{:S(2)}, u32[]{:S(2)}) collective-permute-start(bf16[4,128,512]{2,1,0:T(8,128)(2,1)S(1)} %get-tuple-element.84), channel_id=1, source_target_pairs={{0,1},{1,0},{2,3},{3,2},{4,5},{5,4},{6,7},{7,6},{8,9},{9,8},{10,11... | collective-permute-start | bytes 1572872 | tf_op jit(solution)/shard_map/ppermute | solution.py:60
  84.4 9.2 %collective-permute-start.21 = (bf16[4,128,512]{2,1,0:T(8,128)(2,1)S(1)}, bf16[4,128,512]{2,1,0:T(8,128)(2,1)S(1)}, u32[]{:S(2)}, u32[]{:S(2)}) collective-permute-start(bf16[4,128,512]{2,1,0:T(8,128)(2,1)S(1)} %get-tuple-element.87), channel_id=1, source_target_pairs={{0,6},{1,97},{2,0},{3,99},{4,2},{5,101},{6,4},{7,103},{8,14},{9,10... | collective-permute-start | bytes 1572872 | tf_op jit(solution)/shard_map/ppermute | solution.py:60
  85.0 16.0 %collective-permute-start.19 = (bf16[4,128,512]{2,1,0:T(8,128)(2,1)S(1)}, bf16[4,128,512]{2,1,0:T(8,128)(2,1)S(1)}, u32[]{:S(2)}, u32[]{:S(2)}) collective-permute-start(bf16[4,128,512]{2,1,0:T(8,128)(2,1)S(1)} %get-tuple-element.86), channel_id=1, source_target_pairs={{0,2},{1,33},{2,4},{3,35},{4,6},{5,37},{6,0},{7,39},{8,10},{9,41},... | collective-permute-start | bytes 1572872 | tf_op jit(solution)/shard_map/ppermute | solution.py:60
  86.5 14.5 %collective-permute-start.20 = (bf16[4,128,512]{2,1,0:T(8,128)(2,1)S(1)}, bf16[4,128,512]{2,1,0:T(8,128)(2,1)S(1)}, u32[]{:S(2)}, u32[]{:S(2)}) collective-permute-start(bf16[4,128,512]{2,1,0:T(8,128)(2,1)S(1)} %get-tuple-element.81), channel_id=1, source_target_pairs={{0,4},{1,65},{2,6},{3,67},{4,0},{5,69},{6,2},{7,71},{8,12},{9,73},... | collective-permute-start | bytes 1572872 | tf_op jit(solution)/shard_map/ppermute | solution.py:60
  101.2 10.5 %collective-permute-start.22 = (f32[128,512]{1,0:T(8,128)S(1)}, f32[128,512]{1,0:T(8,128)S(1)}, u32[]{:S(2)}, u32[]{:S(2)}) collective-permute-start(f32[128,512]{1,0:T(8,128)S(1)} %get-tuple-element.89), channel_id=1, source_target_pairs={{0,32},{1,3},{2,34},{3,5},{4,36},{5,7},{6,38},{7,1},{8,40},{9,11},... | collective-permute-start | bytes 786440 | tf_op jit(solution)/shard_map/ppermute | solution.py:60
  101.6 10.1 %collective-permute-start.23 = (f32[128,512]{1,0:T(8,128)S(1)}, f32[128,512]{1,0:T(8,128)S(1)}, u32[]{:S(2)}, u32[]{:S(2)}) collective-permute-start(f32[128,512]{1,0:T(8,128)S(1)} %get-tuple-element.90), channel_id=1, source_target_pairs={{0,64},{1,5},{2,66},{3,7},{4,68},{5,1},{6,70},{7,3},{8,72},{9,13},... | collective-permute-start | bytes 786440 | tf_op jit(solution)/shard_map/ppermute | solution.py:60
  103.8 8.8 %collective-permute-start.24 = (f32[128,512]{1,0:T(8,128)S(1)}, f32[128,512]{1,0:T(8,128)S(1)}, u32[]{:S(2)}, u32[]{:S(2)}) collective-permute-start(f32[128,512]{1,0:T(8,128)S(1)} %get-tuple-element.91), channel_id=1, source_target_pairs={{0,96},{1,7},{2,98},{3,1},{4,100},{5,3},{6,102},{7,5},{8,104},{9,1... | collective-permute-start | bytes 786440 | tf_op jit(solution)/shard_map/ppermute | solution.py:60
  (4 other events, 12.7 us)
